TPU v7x, 1024 devices: a whole 4x4x32 slice. The times are simulated.
1024 devices in a mesh: grp: 16 (over x, y), dev: 64 (over z, core).
Axes of the slice: x: 4, y: 4, z: 32, core: 2. Of those that a mesh axis runs over, the one named last changes fastest.
Arguments:
- papers: bfloat16 [262144, 768], P(('grp', 'dev')), may hold values from -6 to 6
- authors: bfloat16 [262144, 768], P(('grp', 'dev')), may hold values from -6 to 6
- cotangent: bfloat16 [262144, 512], P(('grp', 'dev')), may hold values from -6 to 6
- w_self: bfloat16 [768, 512], replicated, may hold values from -0.21875 to 0.21875
- w_cite: bfloat16 [768, 512], replicated, may hold values from -0.21875 to 0.21875
- w_aut: bfloat16 [768, 512], replicated, may hold values from -0.21875 to 0.21875
- bias: float32 [512], replicated, may hold values from -3 to 3
- cite_col: int32 [262144, 8], P(('grp', 'dev')), may hold values from 0 to 383
- edge_author: int32 [262144], P(('grp', 'dev')), may hold values from 0 to 255
- edge_dest: int32 [262144, 1], P(('grp', 'dev')), may hold values from 0 to 63; in each aligned block of 256 rows (0 to 255, 256 to 511, ...) at most 8 rows name the same one
- edge_row: int32 [262144], P(('grp', 'dev')), may hold values from 0 to 255
Outputs:
- updated: bfloat16 [262144, 512], P(('grp', 'dev'))
- grad_authors: bfloat16 [262144, 768], P(('grp', 'dev'))
- grad_w_aut: float32 [768, 512], replicated
Inputs may be any that keep to these rules, and one draw needn't show every extreme that they name: `edge_dest`: among the 256 edges of one device no destination appears more than 8 times, and some destination appears exactly 8 times.
All inputs are finite; a program needn't handle non-finite values.
Results may differ from a plain program's by a relative error of at most 0.0056.
Values may be sent and summed in bfloat16 or wider, within the bound.
No kernel may reach another device: no remote copies, remote signals or barrier semaphores. Data moves between devices by JAX's collectives and lax.ppermute only.
A program may use at most 32 MiB of HBM per device.

v0:
```python
import jax
import jax.numpy as jnp
from jax import lax
from jax.sharding import PartitionSpec as P

RIM = 64
K_CIT = 8


def padded(block, sides, width):
    for axis, dim in sides:
        count = lax.axis_size(axis)
        forward = [(i, i + 1) for i in range(count - 1)]
        backward = [(target, source) for source, target in forward]
        low = lax.ppermute(
            lax.slice_in_dim(block, block.shape[dim] - width, None, axis=dim), axis, forward
        )
        high = lax.ppermute(lax.slice_in_dim(block, 0, width, axis=dim), axis, backward)
        block = jnp.concatenate([low, block, high], axis=dim)
    return block


def per_device(
    papers,
    authors,
    cotangent,
    w_self,
    w_cite,
    w_aut,
    bias,
    cite_col,
    edge_author,
    edge_dest,
    edge_row,
):
    dev_count = lax.axis_size("dev")
    all_count = lax.axis_size("grp") * dev_count
    pap_rows = papers.shape[0]
    aut_rows = authors.shape[0]
    edge_count = edge_author.shape[0]
    slots = 2 * edge_count // dev_count
    total_slots = dev_count * slots
    out_width = w_aut.shape[1]
    dest = edge_dest[:, 0]
    hot_dest = (
        dest[:, None] == lax.broadcasted_iota(jnp.int32, (edge_count, dev_count), 1)
    ).astype(jnp.int32)
    slot_of = jnp.sum((jnp.cumsum(hot_dest, axis=0) - hot_dest) * hot_dest, axis=1)
    position = dest * slots + slot_of
    edge_rows = jnp.take(authors, edge_author, axis=0)
    outgoing = (
        jnp.zeros((total_slots, edge_rows.shape[1]), jnp.bfloat16).at[position].set(edge_rows)
    )
    targets = jnp.full((total_slots,), -1, jnp.int32).at[position].set(edge_row)
    arrived, arrived_rows = (
        lax.all_to_all(
            outgoing.reshape(dev_count, slots, edge_rows.shape[1]),
            "dev",
            split_axis=0,
            concat_axis=0,
            tiled=True,
        ),
        lax.all_to_all(
            targets.reshape(dev_count, slots), "dev", split_axis=0, concat_axis=0, tiled=True
        ),
    )
    extended = padded(papers, (("dev", 0),), RIM)
    ext_rows = extended.shape[0]
    ext_iota = lax.broadcasted_iota(jnp.int32, (pap_rows, ext_rows), 1)
    picks = jnp.zeros((pap_rows, ext_rows), jnp.float32)
    for which in range(K_CIT):
        picks = picks + (cite_col[:, which : which + 1] == ext_iota).astype(jnp.float32)
    cite_sum = jnp.dot(picks.astype(jnp.bfloat16), extended, preferred_element_type=jnp.float32)
    cite_agg = (cite_sum / K_CIT).astype(jnp.bfloat16)
    pre = jnp.dot(papers, w_self, preferred_element_type=jnp.float32)
    pre = pre + jnp.dot(cite_agg, w_cite, preferred_element_type=jnp.float32)
    flat_arrived = arrived.reshape(total_slots, arrived.shape[2])
    messages = jnp.dot(flat_arrived, w_aut, preferred_element_type=jnp.float32).astype(jnp.bfloat16)
    flat_rows = arrived_rows.reshape(total_slots)
    matches = (
        flat_rows[None, :] == lax.broadcasted_iota(jnp.int32, (pap_rows, total_slots), 0)
    ).astype(jnp.bfloat16)
    aut_sum = jnp.dot(matches, messages, preferred_element_type=jnp.float32)
    count = jnp.sum(matches.astype(jnp.float32), axis=1)
    inverse = 1.0 / jnp.maximum(count, 1.0)
    pre = pre + aut_sum * inverse[:, None] + bias[None, :]
    sigma = jax.nn.sigmoid(pre)
    updated = (pre * sigma).astype(jnp.bfloat16)
    delta = cotangent.astype(jnp.float32) * sigma * (1.0 + pre * (1.0 - sigma))
    scaled = delta * inverse[:, None]
    safe_rows = jnp.maximum(flat_rows, 0)
    slot_grad = jnp.where(flat_rows[:, None] >= 0, jnp.take(scaled, safe_rows, axis=0), 0.0).astype(
        jnp.bfloat16
    )
    returned = lax.all_to_all(
        slot_grad.reshape(dev_count, slots, out_width),
        "dev",
        split_axis=0,
        concat_axis=0,
        tiled=True,
    )
    edge_grad = jnp.take(returned.reshape(total_slots, out_width), position, axis=0)
    owners = (
        edge_author[None, :] == lax.broadcasted_iota(jnp.int32, (aut_rows, edge_count), 0)
    ).astype(jnp.bfloat16)
    grad_proj = jnp.dot(owners, edge_grad, preferred_element_type=jnp.float32).astype(jnp.bfloat16)
    grad_authors = jnp.dot(grad_proj, w_aut.T, preferred_element_type=jnp.float32).astype(
        jnp.bfloat16
    )
    partial_grad = jnp.einsum("ad,ah->dh", authors, grad_proj, preferred_element_type=jnp.float32)
    summed = lax.psum(partial_grad, ("grp", "dev"))
    grad_w_aut = summed / jnp.sqrt(jnp.float32(all_count * aut_rows))
    return (updated, grad_authors, grad_w_aut)


def solution(mesh):
    placed = (
        P(("grp", "dev"), None),
        P(("grp", "dev"), None),
        P(("grp", "dev"), None),
        P(),
        P(),
        P(),
        P(),
        P(("grp", "dev"), None),
        P(("grp", "dev")),
        P(("grp", "dev"), None),
        P(("grp", "dev")),
    )
    return jax.shard_map(
        per_device,
        mesh=mesh,
        in_specs=placed,
        out_specs=(P(("grp", "dev"), None), P(("grp", "dev"), None), P()),
        check_vma=False,
    )
```

profile of v0, /device:TPU:1, one launch (start us, length us, event | category | flops | bytes accessed | tf_op | source)
XLA Modules:
  0.0 1126.3 jit_solution(10750343681319137274)
XLA Ops:
  7.2 0.8 fusion.50
  7.9 0.6 reduce-window.6
  8.8 0.8 fusion.49
  9.6 0.7 and_reduce_fusion
  10.3 1.6 scatter_custom_fusion
  11.8 0.7 all_to_all.12
  12.5 30.4 %all-to-all-start = ((s32[64,1,8]{2,1,0:T(1,128)}), s32[64,1,8]{2,1,0:T(1,128)S(1)}, u32[]{:S(2)}, u32[]{:S(2)}) async-start(s32[64,1,8]{2,1,0:T(1,128)} %bitcast.13), calls=%async_computation | async-start | bytes 65536 | tf_op jit(solution)/shard_map/all_to_all | solution.py:63
  43.0 0.7 compare_select_fusion.1
  43.6 0.7 compare_and_fusion
  44.4 5.1 scatter_custom_fusion.1
  49.4 15.9 %all-to-all-done = s32[64,1,8]{2,1,0:T(1,128)S(1)} async-done(((s32[64,1,8]{2,1,0:T(1,128)}), s32[64,1,8]{2,1,0:T(1,128)S(1)}, u32[]{:S(2)}, u32[]{:S(2)}) %all-to-all-start) | async-done | bytes 2080 | tf_op jit(solution)/shard_map/all_to_all | solution.py:63
  65.3 6.4 all-to-all-start.1
  71.7 3.5 collective-permute-start
  75.3 1.9 collective-permute-start.1
  77.3 0.4 fusion.62
  77.6 0.5 broadcast.122
  78.1 0.7 reduce.7
  79.6 78.5 %all-to-all-done.1 = bf16[64,8,768]{2,1,0:T(8,128)(2,1)S(1)} async-done(((bf16[64,8,768]{2,1,0:T(8,128)(2,1)}), bf16[64,8,768]{2,1,0:T(8,128)(2,1)S(1)}, u32[]{:S(2)}, u32[]{:S(2)}) %all-to-all-start.1) | async-done | bytes 786464 | tf_op jit(solution)/shard_map/all_to_all | solution.py:56
  158.1 1.6 fusion.4
  159.7 3.1 multiply_convert_fusion
  162.8 0.2 multiply_multiply_fusion
  163.1 2.0 gather_fusion
  165.1 1.0 fusion.6
  166.1 6.2 all-to-all-start.2
  172.4 64.3 %all-to-all-done.2 = bf16[64,8,512]{2,1,0:T(8,128)(2,1)S(1)} async-done(((bf16[64,8,512]{2,1,0:T(8,128)(2,1)}), bf16[64,8,512]{2,1,0:T(8,128)(2,1)S(1)}, u32[]{:S(2)}, u32[]{:S(2)}) %all-to-all-start.2) | async-done | bytes 524320 | tf_op jit(solution)/shard_map/all_to_all | solution.py:95
  236.7 1.2 gather_fusion.1
  237.9 0.3 convolution_convert_fusion.2
  238.2 1.6 convolution_bitcast_fusion
  239.8 1.1 convolution_convert_fusion.1
  240.9 875.4 %all-reduce.2.cloned.1.call-done = f32[768,512]{0,1:T(8,128)} async-done(((f32[768,512]{0,1:T(8,128)}), f32[768,512]{0,1:T(8,128)}) %all-reduce.2.cloned.1.call-update) | async-done | bytes 1572880 | tf_op jit(solution)/shard_map/psum | solution.py:111
  1116.3 1.5 broadcast_multiply_fusion
  1117.8 1.6 copy.35
  (38 shorter events, 1.1 us)
Async XLA Ops:
  7.2 151.0 %copy-start = (bf16[768,512]{1,0:T(8,128)(2,1)S(1)}, bf16[768,512]{1,0:T(8,128)(2,1)}, u32[]{:S(2)}) copy-start(bf16[768,512]{1,0:T(8,128)(2,1)} %param.16) | copy-start | bytes 2359300
  7.9 63.8 %copy-start.2 = (bf16[256,768]{1,0:T(8,128)(2,1)S(1)}, bf16[256,768]{1,0:T(8,128)(2,1)}, u32[]{:S(2)}) copy-start(bf16[256,768]{1,0:T(8,128)(2,1)} %param.11) | copy-start | bytes 1179652
  12.5 52.8 %all-to-all-start = ((s32[64,1,8]{2,1,0:T(1,128)}), s32[64,1,8]{2,1,0:T(1,128)S(1)}, u32[]{:S(2)}, u32[]{:S(2)}) async-start(s32[64,1,8]{2,1,0:T(1,128)} %bitcast.13), calls=%async_computation | async-start | bytes 65536 | tf_op jit(solution)/shard_map/all_to_all | solution.py:63
  44.3 32.9 %copy-start.5 = (s32[256,8]{0,1:T(8,128)S(1)}, s32[256,8]{0,1:T(8,128)}, u32[]{:S(2)}) copy-start(s32[256,8]{0,1:T(8,128)} %param.18) | copy-start | bytes 24580
  44.3 32.9 %copy-start.3 = (bf16[768,512]{1,0:T(8,128)(2,1)S(1)}, bf16[768,512]{1,0:T(8,128)(2,1)}, u32[]{:S(2)}) copy-start(bf16[768,512]{1,0:T(8,128)(2,1)} %param.14) | copy-start | bytes 2359300
  65.3 92.8 %all-to-all-start.1 = ((bf16[64,8,768]{2,1,0:T(8,128)(2,1)}), bf16[64,8,768]{2,1,0:T(8,128)(2,1)S(1)}, u32[]{:S(2)}, u32[]{:S(2)}) async-start(bf16[64,8,768]{2,1,0:T(8,128)(2,1)} %bitcast.14), calls=%async_computation.1 | async-start | bytes 1572864 | tf_op jit(solution)/shard_map/all_to_all | solution.py:56
  71.7 88.0 %collective-permute-start = (bf16[64,768]{1,0:T(8,128)(2,1)S(1)}, bf16[64,768]{1,0:T(8,128)(2,1)}, u32[]{:S(2)}, u32[]{:S(2)}) collective-permute-start(bf16[64,768]{1,0:T(8,128)(2,1)S(1)} %get-tuple-element.20), channel_id=1, source_target_pairs={{0,1},{1,2},{2,3},{3,4},{4,5},{5,6},{6,7},{7,8},{8,9},{9,10},{10,1... | collective-permute-start | bytes 294920 | tf_op jit(solution)/shard_map/ppermute | solution.py:15
  75.3 84.4 %collective-permute-start.1 = (bf16[64,768]{1,0:T(8,128)(2,1)S(1)}, bf16[64,768]{1,0:T(8,128)(2,1)}, u32[]{:S(2)}, u32[]{:S(2)}) collective-permute-start(bf16[64,768]{1,0:T(8,128)(2,1)S(1)} %get-tuple-element.21), channel_id=1, source_target_pairs={{1,0},{2,1},{3,2},{4,3},{5,4},{6,5},{7,6},{8,7},{9,8},{10,9},{11,1... | collective-permute-start | bytes 294920 | tf_op jit(solution)/shard_map/ppermute | solution.py:18
  79.6 80.1 %copy-start.7 = (f32[512]{0:T(512)S(1)}, f32[512]{0:T(512)}, u32[]{:S(2)}) copy-start(f32[512]{0:T(512)} %param.17) | copy-start | bytes 6148
  159.7 3.1 copy-start.4
  166.1 71.8 %copy-start.6 = (s32[256]{0:T(256)S(1)}, s32[256]{0:T(256)}, u32[]{:S(2)}) copy-start(s32[256]{0:T(256)} %param.19) | copy-start | bytes 3076
  166.1 70.6 %all-to-all-start.2 = ((bf16[64,8,512]{2,1,0:T(8,128)(2,1)}), bf16[64,8,512]{2,1,0:T(8,128)(2,1)S(1)}, u32[]{:S(2)}, u32[]{:S(2)}) async-start(bf16[64,8,512]{2,1,0:T(8,128)(2,1)} %fusion.6), calls=%async_computation.2 | async-start | bytes 1048576 | tf_op jit(solution)/shard_map/all_to_all | solution.py:95
  172.3 65.9 %copy-start.1 = (bf16[256,768]{1,0:T(8,128)(2,1)S(1)}, bf16[256,768]{1,0:T(8,128)(2,1)}, u32[]{:S(2)}) copy-start(bf16[256,768]{1,0:T(8,128)(2,1)} %param.12) | copy-start | bytes 1179652
  172.3 944.0 %all-reduce.2.cloned.1.call-start = ((), (), s32[]{:S(2)}) async-start(), calls=%async_computation.3 | async-start | bytes 3145728 | tf_op jit(solution)/shard_map/psum | solution.py:111
Sparse Core Ops, SparseCore 0:
  239.9 876.3 all-reduce.1
where the time goes:
time: 1130 us
  waiting for transfers between devices  1030 us (91%)
  starting transfers between devices  48.5 us (4%)
  between operations  14.3 us (1%)
  other arithmetic  13 us (1%)
    psum x1, waiting for transfers between devices, per_device(): summed = lax.psum(partial_grad, ('grp', 'dev'))  875 us
    all_to_all x1, waiting for transfers between devices, per_device(): lax.all_to_all(outgoing.reshape(dev_count, slots, edge_rows.shape[1]), 'd...  78.5 us
    all_to_all x1, waiting for transfers between devices, per_device(): lax.all_to_all(slot_grad.reshape(dev_count, slots, out_width), 'dev', spl...  64.3 us
    all_to_all x1, starting transfers between devices, per_device(): lax.all_to_all(targets.reshape(dev_count, slots), 'dev', split_axis=0, co...  30.4 us
  transfers between devices with their start and end apart: 6, of which 4 were waited for; matrix products, arithmetic and copies ran while one was open for 1% of the time, Pallas kernels for 0%

commit v1 on v0

v1 whole, which is shorter than its diff:
```python
import functools
import math

import jax
import jax.numpy as jnp
from jax import lax
from jax.experimental import pallas as pl
from jax.experimental.pallas import tpu as pltpu
from jax.sharding import PartitionSpec as P

RIM = 64
K_CIT = 8
AUX = 128
BF = jnp.bfloat16
F32 = jnp.float32
NN = (((1,), (0,)), ((), ()))
NT = (((1,), (1,)), ((), ()))
TN = (((0,), (0,)), ((), ()))


def mm(a, b, dims):
    return lax.dot_general(a, b, dims, preferred_element_type=F32)


def call(kernel, outs, args, flops):
    moved = sum(math.prod(a.shape) * a.dtype.itemsize for a in list(args) + list(outs))
    return pl.pallas_call(
        kernel,
        out_shape=outs,
        compiler_params=pltpu.CompilerParams(vmem_limit_bytes=24 * 1024 * 1024),
        cost_estimate=pl.CostEstimate(flops=flops, bytes_accessed=moved, transcendentals=0),
    )(*args)


def pack_kernel(devs, authors, author, dest, row, out, owner):
    edges = author.shape[1]
    auts = authors.shape[0]
    width = authors.shape[1]
    total = out.shape[0]
    cap = total // devs
    dest_of = dest[...]
    hot = (lax.broadcasted_iota(jnp.int32, (devs, edges), 0) == dest_of).astype(F32)
    before = (
        lax.broadcasted_iota(jnp.int32, (edges, edges), 0)
        < lax.broadcasted_iota(jnp.int32, (edges, edges), 1)
    ).astype(F32)
    earlier = mm(hot.astype(BF), before.astype(BF), NN)
    rank = jnp.sum(hot * earlier, axis=0, keepdims=True)
    position = dest_of * cap + rank.astype(jnp.int32)
    slot_edge = (
        (lax.broadcasted_iota(jnp.int32, (total, edges), 0) == position).astype(F32).astype(BF)
    )
    author_edge = (
        (lax.broadcasted_iota(jnp.int32, (auts, edges), 0) == author[...]).astype(F32).astype(BF)
    )
    slot_author = mm(slot_edge, author_edge, NT).astype(BF)
    owner[...] = slot_author
    out[:, :width] = mm(slot_author, authors[...], NN).astype(BF)
    lane = lax.broadcasted_iota(jnp.int32, (AUX, edges), 0)
    aux = jnp.where(lane == 0, row[...] + 1, jnp.where(lane == 1, 1, 0)).astype(F32).astype(BF)
    out[:, width:] = mm(slot_edge, aux, NT).astype(BF)


def base_kernel(papers, low, high, cite, w_self, w_cite, bias, base):
    rows = papers.shape[0]
    ext = rows + 2 * RIM
    column = lax.broadcasted_iota(jnp.int32, (ext, rows), 0)
    picks = jnp.zeros((ext, rows), F32)
    for which in range(K_CIT):
        picks = picks + (column == cite[which : which + 1, :]).astype(F32)
    picks = picks.astype(BF)
    cites = mm(picks[:RIM], low[...], TN)
    cites = cites + mm(picks[RIM : RIM + rows], papers[...], TN)
    cites = cites + mm(picks[RIM + rows :], high[...], TN)
    cite_agg = (cites * (1.0 / K_CIT)).astype(BF)
    pre = mm(papers[...], w_self[...], NN)
    base[...] = pre + mm(cite_agg, w_cite[...], NN) + bias[...]


def node_kernel(arrived, base, cotangent, w_aut, updated, slot_grad):
    total = arrived.shape[0]
    rows = base.shape[0]
    width = w_aut.shape[0]
    aux = arrived[:, width:]
    row_of = aux[:, :1].astype(F32)
    wanted = lax.broadcasted_iota(jnp.int32, (total, rows), 1).astype(F32) + 1.0
    match = (row_of == wanted).astype(F32).astype(BF)
    messages = mm(arrived[:, :width], w_aut[...], NN).astype(BF)
    aut_sum = mm(match, messages, TN)
    count = mm(match, aux, TN)[:, 1:2]
    inverse = 1.0 / jnp.maximum(count, 1.0)
    pre = base[...] + aut_sum * inverse
    sigma = jax.nn.sigmoid(pre)
    updated[...] = (pre * sigma).astype(BF)
    delta = cotangent[...].astype(F32) * sigma * (1.0 + pre * (1.0 - sigma))
    scaled = (delta * inverse).astype(BF)
    slot_grad[...] = mm(match, scaled, NN).astype(BF)


def weight_kernel(arrived, slot_grad, partial):
    width = partial.shape[0]
    partial[...] = mm(arrived[:, :width], slot_grad[...], TN).astype(BF)


def author_kernel(returned, owner, w_aut, grad_authors):
    grad_proj = mm(owner[...], returned[...], TN).astype(BF)
    grad_authors[...] = mm(grad_proj, w_aut[...], NT).astype(BF)


def shift_sum(block, place, count, axis, perm, dim):
    size = block.shape[dim] // count

    def piece(at):
        start = [0] * block.ndim
        start[dim] = at * size
        sizes = list(block.shape)
        sizes[dim] = size
        return lax.dynamic_slice(block, start, sizes, allow_negative_indices=False)

    came = [
        lax.ppermute(piece(lax.rem(place + k, count)), axis, perm(k)) for k in range(1, count)
    ]
    total = piece(place).astype(F32)
    for other in came:
        total = total + other.astype(F32)
    return total


def reduce_weight(partial, grp_count, dev_count):
    side = math.isqrt(grp_count)
    low = 4
    grp = lax.axis_index("grp")
    dev = lax.axis_index("dev")
    x, y = lax.div(grp, side), lax.rem(grp, side)
    z_low, core = (dev >> 1) & (low - 1), dev & 1

    def along_x(k):
        return [(g, (g // side + k) % side * side + g % side) for g in range(grp_count)]

    def along_y(k):
        return [(g, g // side * side + (g % side + k) % side) for g in range(grp_count)]

    def along_core(k):
        return [(d, d ^ 1) for d in range(dev_count)]

    def along_low(k):
        span = 2 * low
        return [(d, d // span * span + (d + 2 * k) % span) for d in range(dev_count)]

    part = shift_sum(partial, x, side, "grp", along_x, 0).astype(BF)
    part = shift_sum(part, y, side, "grp", along_y, 0).astype(BF)
    part = shift_sum(part, core, 2, "dev", along_core, 0)
    part = shift_sum(part, z_low, low, "dev", along_low, 1)
    span = 2 * low
    far = [[b * span + i for b in range(dev_count // span)] for i in range(span)]
    near = [[b * span + i for i in range(span)] for b in range(dev_count // span)]
    rows, lanes = part.shape
    every = lax.all_gather(part, "dev", axis_index_groups=far, axis=0)
    part = jnp.sum(every, axis=0).astype(BF)
    near_all = lax.all_gather(part, "dev", axis_index_groups=near, axis=0)
    near_all = near_all.reshape(low, 2, rows, lanes).transpose(1, 2, 0, 3)
    near_all = near_all.reshape(2 * rows, low * lanes)
    return lax.all_gather(near_all, "grp", axis=0, tiled=True)


def per_device(
    papers,
    authors,
    cotangent,
    w_self,
    w_cite,
    w_aut,
    bias,
    cite_col,
    edge_author,
    edge_dest,
    edge_row,
):
    dev_count = lax.axis_size("dev")
    grp_count = lax.axis_size("grp")
    all_count = grp_count * dev_count
    pap_rows, width = papers.shape
    aut_rows = authors.shape[0]
    edges = edge_author.shape[0]
    slots = 2 * edges // dev_count
    total = dev_count * slots
    hidden = w_aut.shape[1]
    shape = jax.ShapeDtypeStruct

    outgoing, owner = call(
        functools.partial(pack_kernel, dev_count),
        (shape((total, width + AUX), BF), shape((total, aut_rows), BF)),
        (
            authors,
            edge_author.reshape(1, edges),
            edge_dest.reshape(1, edges),
            edge_row.reshape(1, edges),
        ),
        2 * total * aut_rows * (edges + width),
    )
    arrived = lax.all_to_all(
        outgoing.reshape(dev_count, slots, width + AUX), "dev", 0, 0, tiled=True
    ).reshape(total, width + AUX)
    forward = [(i, i + 1) for i in range(dev_count - 1)]
    backward = [(i + 1, i) for i in range(dev_count - 1)]
    low = lax.ppermute(papers[pap_rows - RIM :], "dev", forward)
    high = lax.ppermute(papers[:RIM], "dev", backward)
    (base,) = call(
        base_kernel,
        (shape((pap_rows, hidden), F32),),
        (papers, low, high, cite_col.T, w_self, w_cite, bias.reshape(1, hidden)),
        2 * pap_rows * width * (2 * hidden + pap_rows + 2 * RIM),
    )
    updated, slot_grad = call(
        node_kernel,
        (shape((pap_rows, hidden), BF), shape((total, hidden), BF)),
        (arrived, base, cotangent, w_aut),
        2 * total * hidden * (width + 2 * pap_rows),
    )
    returned = lax.all_to_all(
        slot_grad.reshape(dev_count, slots, hidden), "dev", 0, 0, tiled=True
    ).reshape(total, hidden)
    (partial,) = call(
        weight_kernel,
        (shape((width, hidden), BF),),
        (arrived, slot_grad),
        2 * total * width * hidden,
    )
    summed = reduce_weight(partial, grp_count, dev_count)
    (grad_authors,) = call(
        author_kernel,
        (shape((aut_rows, width), BF),),
        (returned, owner, w_aut),
        2 * aut_rows * hidden * (total + width),
    )
    grad_w_aut = summed.astype(F32) / jnp.sqrt(jnp.float32(all_count * aut_rows))
    return (updated, grad_authors, grad_w_aut)


def solution(mesh):
    placed = (
        P(("grp", "dev"), None),
        P(("grp", "dev"), None),
        P(("grp", "dev"), None),
        P(),
        P(),
        P(),
        P(),
        P(("grp", "dev"), None),
        P(("grp", "dev")),
        P(("grp", "dev"), None),
        P(("grp", "dev")),
    )
    return jax.shard_map(
        per_device,
        mesh=mesh,
        in_specs=placed,
        out_specs=(P(("grp", "dev"), None), P(("grp", "dev"), None), P()),
        check_vma=False,
    )
```

time: 1130 us -> 281 us (0.25)
  waiting for transfers between devices: 1030 us -> 102 us
  blocking collectives: 0 us -> 79.3 us
  starting transfers between devices: 48.5 us -> 79 us
  between operations: 14.3 us -> 1.03 us
  other arithmetic: 13 us -> 1.53 us
    psum x1 -> x0, waiting for transfers between devices: 875 us -> none  [per_device(): summed = lax.psum(partial_grad, ('grp', 'dev'))]
    all_to_all x3 -> x2, waiting for transfers between devices: 159 us -> 15.7 us  [the longest x1 15.7 us: per_device(): lax.all_to_all(outgoing.reshape(dev_count, slots, width + AUX), 'dev', 0,...]
    ppermute x2 -> x12, waiting for transfers between devices: 0.01 us -> 86.1 us  [the longest x1 73.7 us: per_device(): high = lax.ppermute(papers[:RIM], 'dev', backward)]
    all_gather x0 -> x3, blocking collectives: none -> 79.3 us  [the longest x1 38.6 us: reduce_weight(): every = lax.all_gather(part, 'dev', axis_index_groups=far, axis=0)]
    ppermute x2 -> x12, starting transfers between devices: 5.46 us -> 40.4 us  [the longest x10 34.7 us: shift_sum(): lax.ppermute(piece(lax.rem(place + k, count)), axis, perm(k))]
    all_to_all x3 -> x2, starting transfers between devices: 43 us -> 38.6 us  [the longest x1 30.4 us: per_device(): lax.all_to_all(outgoing.reshape(dev_count, slots, width + AUX), 'dev', 0,...]
  transfers between devices with their start and end apart: 6 -> 14, of which waited for: 4 -> 7; matrix products, arithmetic and copies ran while one was open for 1% -> 1% of each run, Pallas kernels for 0% -> 1%
where the time goes in v1:
time: 281 us; the launch traced here: 277 us
  waiting for transfers between devices  102 us (36%)
  blocking collectives  79.3 us (28%)
  starting transfers between devices  79 us (28%)
  Pallas kernels  8 us (3%)
  local copies, waits for them, and re-layouts  6.03 us (2%)
    ppermute x1, waiting for transfers between devices, per_device(): high = lax.ppermute(papers[:RIM], 'dev', backward)  73.7 us
    all_gather x1, blocking collectives, reduce_weight(): every = lax.all_gather(part, 'dev', axis_index_groups=far, axis=0)  38.6 us
    ppermute x10, starting transfers between devices, shift_sum(): lax.ppermute(piece(lax.rem(place + k, count)), axis, perm(k))  34.7 us
    all_to_all x1, starting transfers between devices, per_device(): lax.all_to_all(outgoing.reshape(dev_count, slots, width + AUX), 'dev', 0,...  30.4 us
    all_gather x1, blocking collectives, reduce_weight(): near_all = lax.all_gather(part, 'dev', axis_index_groups=near, axis=0)  22.2 us
    all_gather x1, blocking collectives, reduce_weight(): return lax.all_gather(near_all, 'grp', axis=0, tiled=True)  18.6 us
    all_to_all x1, waiting for transfers between devices, per_device(): lax.all_to_all(outgoing.reshape(dev_count, slots, width + AUX), 'dev', 0,...  15.7 us
    ppermute x10, waiting for transfers between devices, shift_sum(): lax.ppermute(piece(lax.rem(place + k, count)), axis, perm(k))  12.5 us
  transfers between devices with their start and end apart: 14, of which 7 were waited for; matrix products, arithmetic and copies ran while one was open for 1% of the time, Pallas kernels for 1%

profile of v1, /device:TPU:1, one launch (start us, length us, event | category | flops | bytes accessed | tf_op | source)
XLA Modules:
  0.0 276.8 jit_solution(18383378562746045298)
XLA Ops:
  0.7 1.0 copy-done.9
  3.7 1.7 shard_map.130
  6.1 30.4 %all-to-all-start = ((bf16[64,8,896]{2,1,0:T(8,128)(2,1)}), bf16[64,8,896]{2,1,0:T(8,128)(2,1)S(1)}, u32[]{:S(2)}, u32[]{:S(2)}) async-start(bf16[64,8,896]{2,1,0:T(8,128)(2,1)} %bitcast.3), calls=%async_computation | async-start | bytes 1835008 | tf_op jit(solution)/shard_map/all_to_all | solution.py:201
  36.6 2.5 collective-permute-start.1
  39.1 3.2 %collective-permute-start = (bf16[64,768]{1,0:T(8,128)(2,1)S(1)}, bf16[64,768]{1,0:T(8,128)(2,1)S(1)}, u32[]{:S(2)}, u32[]{:S(2)}) collective-permute-start(bf16[64,768]{1,0:T(8,128)(2,1)S(1)} %get-tuple-element.15), channel_id=1, source_target_pairs={{0,1},{1,2},{2,3},{3,4},{4,5},{5,6},{6,7},{7,8},{8,9},{9,10},{10,1... | collective-permute-start | bytes 294920 | tf_op jit(solution)/shard_map/ppermute | solution.py:206
  42.3 73.7 %collective-permute-done.1.high = bf16[64,768]{1,0:T(8,128)(2,1)S(1)} collective-permute-done((bf16[64,768]{1,0:T(8,128)(2,1)S(1)}, bf16[64,768]{1,0:T(8,128)(2,1)S(1)}, u32[]{:S(2)}, u32[]{:S(2)}) %collective-permute-start.1) | collective-permute-done | bytes 98336 | tf_op jit(solution)/shard_map/ppermute | solution.py:207
  116.0 1.1 copy-done.3
  117.1 1.1 shard_map.131.base
  118.2 15.7 %all-to-all-done = bf16[64,8,896]{2,1,0:T(8,128)(2,1)S(1)} async-done(((bf16[64,8,896]{2,1,0:T(8,128)(2,1)}), bf16[64,8,896]{2,1,0:T(8,128)(2,1)S(1)}, u32[]{:S(2)}, u32[]{:S(2)}) %all-to-all-start) | async-done | bytes 917536 | tf_op jit(solution)/shard_map/all_to_all | solution.py:201
  133.9 0.9 copy-done.4
  134.9 2.2 shard_map.132
  137.0 8.2 %all-to-all-start.1 = ((bf16[64,8,512]{2,1,0:T(8,128)(2,1)}), bf16[64,8,512]{2,1,0:T(8,128)(2,1)S(1)}, u32[]{:S(2)}, u32[]{:S(2)}) async-start(bf16[64,8,512]{2,1,0:T(8,128)(2,1)} %bitcast.7), calls=%async_computation.1 | async-start | bytes 1048576 | tf_op jit(solution)/shard_map/all_to_all | solution.py:220
  145.3 1.7 shard_map.134
  147.1 3.1 %collective-permute-start.2 = (bf16[192,512]{1,0:T(8,128)(2,1)S(1)}, bf16[192,512]{1,0:T(8,128)(2,1)S(1)}, u32[]{:S(2)}, u32[]{:S(2)}) collective-permute-start(bf16[192,512]{1,0:T(8,128)(2,1)S(1)} %get-tuple-element.11), channel_id=1, source_target_pairs={{0,256},{64,320},{128,384},{192,448},{256,512},{320,576},{384,640}... | collective-permute-start | bytes 589832 | tf_op jit(solution)/shard_map/ppermute | solution.py:121
  150.2 3.4 %collective-permute-start.4 = (bf16[192,512]{1,0:T(8,128)(2,1)S(1)}, bf16[192,512]{1,0:T(8,128)(2,1)S(1)}, u32[]{:S(2)}, u32[]{:S(2)}) collective-permute-start(bf16[192,512]{1,0:T(8,128)(2,1)S(1)} %get-tuple-element.12), channel_id=1, source_target_pairs={{0,768},{64,832},{128,896},{192,960},{256,0},{320,64},{384,128},{4... | collective-permute-start | bytes 589832 | tf_op jit(solution)/shard_map/ppermute | solution.py:121
  153.6 3.4 %collective-permute-start.3 = (bf16[192,512]{1,0:T(8,128)(2,1)S(1)}, bf16[192,512]{1,0:T(8,128)(2,1)S(1)}, u32[]{:S(2)}, u32[]{:S(2)}) collective-permute-start(bf16[192,512]{1,0:T(8,128)(2,1)S(1)} %get-tuple-element.13), channel_id=1, source_target_pairs={{0,512},{64,576},{128,640},{192,704},{256,768},{320,832},{384,896}... | collective-permute-start | bytes 589832 | tf_op jit(solution)/shard_map/ppermute | solution.py:121
  157.8 4.6 %collective-permute-done.3 = bf16[192,512]{1,0:T(8,128)(2,1)S(1)} collective-permute-done((bf16[192,512]{1,0:T(8,128)(2,1)S(1)}, bf16[192,512]{1,0:T(8,128)(2,1)S(1)}, u32[]{:S(2)}, u32[]{:S(2)}) %collective-permute-start.3) | collective-permute-done | bytes 196640 | tf_op jit(solution)/shard_map/ppermute | solution.py:121
  162.5 3.2 %collective-permute-start.5 = (bf16[48,512]{1,0:T(8,128)(2,1)S(1)}, bf16[48,512]{1,0:T(8,128)(2,1)S(1)}, u32[]{:S(2)}, u32[]{:S(2)}) collective-permute-start(bf16[48,512]{1,0:T(8,128)(2,1)S(1)} %get-tuple-element.16), channel_id=1, source_target_pairs={{0,64},{64,128},{128,192},{192,0},{256,320},{320,384},{384,448},{4... | collective-permute-start | bytes 147464 | tf_op jit(solution)/shard_map/ppermute | solution.py:121
  165.7 3.4 %collective-permute-start.7 = (bf16[48,512]{1,0:T(8,128)(2,1)S(1)}, bf16[48,512]{1,0:T(8,128)(2,1)S(1)}, u32[]{:S(2)}, u32[]{:S(2)}) collective-permute-start(bf16[48,512]{1,0:T(8,128)(2,1)S(1)} %get-tuple-element.17), channel_id=1, source_target_pairs={{0,192},{64,0},{128,64},{192,128},{256,448},{320,256},{384,320},{4... | collective-permute-start | bytes 147464 | tf_op jit(solution)/shard_map/ppermute | solution.py:121
  169.1 3.5 %collective-permute-start.6 = (bf16[48,512]{1,0:T(8,128)(2,1)S(1)}, bf16[48,512]{1,0:T(8,128)(2,1)S(1)}, u32[]{:S(2)}, u32[]{:S(2)}) collective-permute-start(bf16[48,512]{1,0:T(8,128)(2,1)S(1)} %get-tuple-element.18), channel_id=1, source_target_pairs={{0,128},{64,192},{128,0},{192,64},{256,384},{320,448},{384,256},{4... | collective-permute-start | bytes 147464 | tf_op jit(solution)/shard_map/ppermute | solution.py:121
  172.6 3.1 %collective-permute-done.6 = bf16[48,512]{1,0:T(8,128)(2,1)S(1)} collective-permute-done((bf16[48,512]{1,0:T(8,128)(2,1)S(1)}, bf16[48,512]{1,0:T(8,128)(2,1)S(1)}, u32[]{:S(2)}, u32[]{:S(2)}) %collective-permute-start.6) | collective-permute-done | bytes 49184 | tf_op jit(solution)/shard_map/ppermute | solution.py:121
  175.8 5.2 %collective-permute-start.8 = (bf16[24,512]{1,0:T(8,128)(2,1)S(1)}, bf16[24,512]{1,0:T(8,128)(2,1)S(1)}, u32[]{:S(2)}, u32[]{:S(2)}) collective-permute-start(bf16[24,512]{1,0:T(8,128)(2,1)S(1)} %constant_dynamic-slice_fusion.3), channel_id=1, source_target_pairs={{0,1},{1,0},{2,3},{3,2},{4,5},{5,4},{6,7},{7,6},{8,9},{9,8},{10,11... | collective-permute-start | bytes 73736 | tf_op jit(solution)/shard_map/ppermute | solution.py:121
  181.0 0.8 collective-permute-done.8
  181.8 3.3 %collective-permute-start.9 = (f32[24,128]{1,0:T(8,128)S(1)}, f32[24,128]{1,0:T(8,128)S(1)}, u32[]{:S(2)}, u32[]{:S(2)}) collective-permute-start(f32[24,128]{1,0:T(8,128)S(1)} %get-tuple-element.19), channel_id=1, source_target_pairs={{0,2},{1,3},{2,4},{3,5},{4,6},{5,7},{6,0},{7,1},{8,10},{9,11},{10,... | collective-permute-start | bytes 36872 | tf_op jit(solution)/shard_map/ppermute | solution.py:121
  185.1 3.8 %collective-permute-start.11 = (f32[24,128]{1,0:T(8,128)S(1)}, f32[24,128]{1,0:T(8,128)S(1)}, u32[]{:S(2)}, u32[]{:S(2)}) collective-permute-start(f32[24,128]{1,0:T(8,128)S(1)} %get-tuple-element.20), channel_id=1, source_target_pairs={{0,6},{1,7},{2,0},{3,1},{4,2},{5,3},{6,4},{7,5},{8,14},{9,15},{10,... | collective-permute-start | bytes 36872 | tf_op jit(solution)/shard_map/ppermute | solution.py:121
  188.9 2.4 collective-permute-start.10
  191.3 3.3 %collective-permute-done.10 = f32[24,128]{1,0:T(8,128)S(1)} collective-permute-done((f32[24,128]{1,0:T(8,128)S(1)}, f32[24,128]{1,0:T(8,128)S(1)}, u32[]{:S(2)}, u32[]{:S(2)}) %collective-permute-start.10) | collective-permute-done | bytes 12320 | tf_op jit(solution)/shard_map/ppermute | solution.py:121
  194.7 38.6 %all-gather = f32[192,128]{1,0:T(8,128)S(1)} all-gather(f32[24,128]{1,0:T(8,128)S(1)} %add_add_fusion), channel_id=2, replica_groups={{0,8,16,24,32,40,48,56},{1,9,17,25,33,41,49,57},{2,10,18,26,34,42,50,58..., dimensions={0}, use_global_device_ids=true | all-gather | bytes 110592 | tf_op jit(solution)/shard_map/all_gather | solution.py:158
  233.3 22.2 %all-gather.1 = bf16[192,128]{1,0:T(8,128)(2,1)S(1)} all-gather(bf16[24,128]{1,0:T(8,128)(2,1)S(1)} %reduce_sum.9), channel_id=3, replica_groups={{0,1,2,3,4,5,6,7},{8,9,10,11,12,13,14,15},{16,17,18,19,20,21,22,23},{24..., dimensions={0}, use_global_device_ids=true | all-gather | bytes 55296 | tf_op jit(solution)/shard_map/all_gather | solution.py:160
  255.5 18.6 %all_gather.16 = bf16[768,512]{1,0:T(8,128)(2,1)S(1)} all-gather(bf16[48,512]{1,0:T(8,128)(2,1)S(1)} %bitcast.27), channel_id=1, replica_groups=mesh['grp'=16,'dev'=64] {'grp'}, dimensions={0}, use_global_device_ids=true | all-gather | bytes 835584 | tf_op jit(solution)/shard_map/all_gather | solution.py:163
  274.1 1.4 convert_multiply_fusion
  275.4 1.4 shard_map.133
  (43 shorter events, 3.8 us)
Async XLA Ops:
  0.6 35.9 %copy-start.1 = (bf16[256,768]{1,0:T(8,128)(2,1)S(1)}, bf16[256,768]{1,0:T(8,128)(2,1)}, u32[]{:S(2)}) copy-start(bf16[256,768]{1,0:T(8,128)(2,1)} %papers.1) | copy-start | bytes 1179652
  0.6 1.0 copy-start.9
  1.7 0.7 copy-start.10
  2.4 0.7 copy-start.11
  3.0 0.7 copy-start.12
  3.7 112.2 %copy-start.2 = (bf16[768,512]{1,0:T(8,128)(2,1)S(1)}, bf16[768,512]{1,0:T(8,128)(2,1)}, u32[]{:S(2)}) copy-start(bf16[768,512]{1,0:T(8,128)(2,1)} %w_self.1) | copy-start | bytes 2359300
  3.7 112.2 %copy-start.7 = (s32[256,8]{0,1:T(8,128)S(1)}, s32[256,8]{0,1:T(8,128)}, u32[]{:S(2)}) copy-start(s32[256,8]{0,1:T(8,128)} %param.18) | copy-start | bytes 24580
  3.7 112.2 %copy-start.8 = (f32[512]{0:T(512)S(1)}, f32[512]{0:T(512)}, u32[]{:S(2)}) copy-start(f32[512]{0:T(512)} %param.17) | copy-start | bytes 6148
  5.4 0.7 copy-start.5
  6.1 127.8 %all-to-all-start = ((bf16[64,8,896]{2,1,0:T(8,128)(2,1)}), bf16[64,8,896]{2,1,0:T(8,128)(2,1)S(1)}, u32[]{:S(2)}, u32[]{:S(2)}) async-start(bf16[64,8,896]{2,1,0:T(8,128)(2,1)} %bitcast.3), calls=%async_computation | async-start | bytes 1835008 | tf_op jit(solution)/shard_map/all_to_all | solution.py:201
  36.5 97.4 %copy-start = (bf16[768,512]{1,0:T(8,128)(2,1)S(1)}, bf16[768,512]{1,0:T(8,128)(2,1)}, u32[]{:S(2)}) copy-start(bf16[768,512]{1,0:T(8,128)(2,1)} %w_aut.3) | copy-start | bytes 2359300
  36.6 79.4 %collective-permute-start.1 = (bf16[64,768]{1,0:T(8,128)(2,1)S(1)}, bf16[64,768]{1,0:T(8,128)(2,1)S(1)}, u32[]{:S(2)}, u32[]{:S(2)}) collective-permute-start(bf16[64,768]{1,0:T(8,128)(2,1)S(1)} %get-tuple-element.14), channel_id=1, source_target_pairs={{1,0},{2,1},{3,2},{4,3},{5,4},{6,5},{7,6},{8,7},{9,8},{10,9},{11,1... | collective-permute-start | bytes 294920 | tf_op jit(solution)/shard_map/ppermute | solution.py:207
  39.1 76.9 %collective-permute-start = (bf16[64,768]{1,0:T(8,128)(2,1)S(1)}, bf16[64,768]{1,0:T(8,128)(2,1)S(1)}, u32[]{:S(2)}, u32[]{:S(2)}) collective-permute-start(bf16[64,768]{1,0:T(8,128)(2,1)S(1)} %get-tuple-element.15), channel_id=1, source_target_pairs={{0,1},{1,2},{2,3},{3,4},{4,5},{5,6},{6,7},{7,8},{8,9},{9,10},{10,1... | collective-permute-start | bytes 294920 | tf_op jit(solution)/shard_map/ppermute | solution.py:206
  116.0 1.1 copy-start.3
  133.9 1.0 copy-start.4
  137.0 138.4 %all-to-all-start.1 = ((bf16[64,8,512]{2,1,0:T(8,128)(2,1)}), bf16[64,8,512]{2,1,0:T(8,128)(2,1)S(1)}, u32[]{:S(2)}, u32[]{:S(2)}) async-start(bf16[64,8,512]{2,1,0:T(8,128)(2,1)} %bitcast.7), calls=%async_computation.1 | async-start | bytes 1048576 | tf_op jit(solution)/shard_map/all_to_all | solution.py:220
  147.1 10.0 %collective-permute-start.2 = (bf16[192,512]{1,0:T(8,128)(2,1)S(1)}, bf16[192,512]{1,0:T(8,128)(2,1)S(1)}, u32[]{:S(2)}, u32[]{:S(2)}) collective-permute-start(bf16[192,512]{1,0:T(8,128)(2,1)S(1)} %get-tuple-element.11), channel_id=1, source_target_pairs={{0,256},{64,320},{128,384},{192,448},{256,512},{320,576},{384,640}... | collective-permute-start | bytes 589832 | tf_op jit(solution)/shard_map/ppermute | solution.py:121
  150.2 7.6 %collective-permute-start.4 = (bf16[192,512]{1,0:T(8,128)(2,1)S(1)}, bf16[192,512]{1,0:T(8,128)(2,1)S(1)}, u32[]{:S(2)}, u32[]{:S(2)}) collective-permute-start(bf16[192,512]{1,0:T(8,128)(2,1)S(1)} %get-tuple-element.12), channel_id=1, source_target_pairs={{0,768},{64,832},{128,896},{192,960},{256,0},{320,64},{384,128},{4... | collective-permute-start | bytes 589832 | tf_op jit(solution)/shard_map/ppermute | solution.py:121
  153.6 8.8 %collective-permute-start.3 = (bf16[192,512]{1,0:T(8,128)(2,1)S(1)}, bf16[192,512]{1,0:T(8,128)(2,1)S(1)}, u32[]{:S(2)}, u32[]{:S(2)}) collective-permute-start(bf16[192,512]{1,0:T(8,128)(2,1)S(1)} %get-tuple-element.13), channel_id=1, source_target_pairs={{0,512},{64,576},{128,640},{192,704},{256,768},{320,832},{384,896}... | collective-permute-start | bytes 589832 | tf_op jit(solution)/shard_map/ppermute | solution.py:121
  162.5 10.1 %collective-permute-start.5 = (bf16[48,512]{1,0:T(8,128)(2,1)S(1)}, bf16[48,512]{1,0:T(8,128)(2,1)S(1)}, u32[]{:S(2)}, u32[]{:S(2)}) collective-permute-start(bf16[48,512]{1,0:T(8,128)(2,1)S(1)} %get-tuple-element.16), channel_id=1, source_target_pairs={{0,64},{64,128},{128,192},{192,0},{256,320},{320,384},{384,448},{4... | collective-permute-start | bytes 147464 | tf_op jit(solution)/shard_map/ppermute | solution.py:121
  165.7 6.9 %collective-permute-start.7 = (bf16[48,512]{1,0:T(8,128)(2,1)S(1)}, bf16[48,512]{1,0:T(8,128)(2,1)S(1)}, u32[]{:S(2)}, u32[]{:S(2)}) collective-permute-start(bf16[48,512]{1,0:T(8,128)(2,1)S(1)} %get-tuple-element.17), channel_id=1, source_target_pairs={{0,192},{64,0},{128,64},{192,128},{256,448},{320,256},{384,320},{4... | collective-permute-start | bytes 147464 | tf_op jit(solution)/shard_map/ppermute | solution.py:121
  169.1 6.6 %collective-permute-start.6 = (bf16[48,512]{1,0:T(8,128)(2,1)S(1)}, bf16[48,512]{1,0:T(8,128)(2,1)S(1)}, u32[]{:S(2)}, u32[]{:S(2)}) collective-permute-start(bf16[48,512]{1,0:T(8,128)(2,1)S(1)} %get-tuple-element.18), channel_id=1, source_target_pairs={{0,128},{64,192},{128,0},{192,64},{256,384},{320,448},{384,256},{4... | collective-permute-start | bytes 147464 | tf_op jit(solution)/shard_map/ppermute | solution.py:121
  175.8 6.0 %collective-permute-start.8 = (bf16[24,512]{1,0:T(8,128)(2,1)S(1)}, bf16[24,512]{1,0:T(8,128)(2,1)S(1)}, u32[]{:S(2)}, u32[]{:S(2)}) collective-permute-start(bf16[24,512]{1,0:T(8,128)(2,1)S(1)} %constant_dynamic-slice_fusion.3), channel_id=1, source_target_pairs={{0,1},{1,0},{2,3},{3,2},{4,5},{5,4},{6,7},{7,6},{8,9},{9,8},{10,11... | collective-permute-start | bytes 73736 | tf_op jit(solution)/shard_map/ppermute | solution.py:121
  181.8 9.5 %collective-permute-start.9 = (f32[24,128]{1,0:T(8,128)S(1)}, f32[24,128]{1,0:T(8,128)S(1)}, u32[]{:S(2)}, u32[]{:S(2)}) collective-permute-start(f32[24,128]{1,0:T(8,128)S(1)} %get-tuple-element.19), channel_id=1, source_target_pairs={{0,2},{1,3},{2,4},{3,5},{4,6},{5,7},{6,0},{7,1},{8,10},{9,11},{10,... | collective-permute-start | bytes 36872 | tf_op jit(solution)/shard_map/ppermute | solution.py:121
  185.1 6.2 %collective-permute-start.11 = (f32[24,128]{1,0:T(8,128)S(1)}, f32[24,128]{1,0:T(8,128)S(1)}, u32[]{:S(2)}, u32[]{:S(2)}) collective-permute-start(f32[24,128]{1,0:T(8,128)S(1)} %get-tuple-element.20), channel_id=1, source_target_pairs={{0,6},{1,7},{2,0},{3,1},{4,2},{5,3},{6,4},{7,5},{8,14},{9,15},{10,... | collective-permute-start | bytes 36872 | tf_op jit(solution)/shard_map/ppermute | solution.py:121
  188.9 5.7 %collective-permute-start.10 = (f32[24,128]{1,0:T(8,128)S(1)}, f32[24,128]{1,0:T(8,128)S(1)}, u32[]{:S(2)}, u32[]{:S(2)}) collective-permute-start(f32[24,128]{1,0:T(8,128)S(1)} %get-tuple-element.21), channel_id=1, source_target_pairs={{0,4},{1,5},{2,6},{3,7},{4,0},{5,1},{6,2},{7,3},{8,12},{9,13},{10,... | collective-permute-start | bytes 36872 | tf_op jit(solution)/shard_map/ppermute | solution.py:121
  255.5 19.9 %copy-start.6 = (bf16[512,256]{1,0:T(8,128)(2,1)S(1)}, bf16[512,256]{1,0:T(8,128)(2,1)}, u32[]{:S(2)}) copy-start(bf16[512,256]{1,0:T(8,128)(2,1)} %copy-done.5) | copy-start | bytes 786436

commit v2 on v1

v2 whole, which is shorter than its diff:
```python
import functools
import math

import jax
import jax.numpy as jnp
from jax import lax
from jax.experimental import pallas as pl
from jax.experimental.pallas import tpu as pltpu
from jax.sharding import PartitionSpec as P

RIM = 64
K_CIT = 8
AUX = 128
HALVES = 2
NEAR = 4
BF = jnp.bfloat16
F32 = jnp.float32
NN = (((1,), (0,)), ((), ()))
NT = (((1,), (1,)), ((), ()))
TN = (((0,), (0,)), ((), ()))


def mm(a, b, dims):
    return lax.dot_general(a, b, dims, preferred_element_type=F32)


def where_equal(a, b):
    return (a == b).astype(F32).astype(BF)


def iota(shape, dim):
    return lax.broadcasted_iota(jnp.int32, shape, dim)


def call(kernel, outs, args, flops):
    moved = sum(math.prod(a.shape) * a.dtype.itemsize for a in list(args) + list(outs))
    return pl.pallas_call(
        kernel,
        out_shape=outs,
        compiler_params=pltpu.CompilerParams(vmem_limit_bytes=16 * 1024 * 1024),
        cost_estimate=pl.CostEstimate(flops=flops, bytes_accessed=moved, transcendentals=0),
    )(*args)


def edge_slots(dest_of, devs, cap):
    edges = dest_of.shape[1]
    hot = (iota((devs, edges), 0) == dest_of).astype(F32)
    before = (iota((edges, edges), 0) < iota((edges, edges), 1)).astype(F32).astype(BF)
    earlier = mm(hot.astype(BF), before, NN)
    rank = jnp.sum(hot * earlier, axis=0, keepdims=True)
    return dest_of * cap + rank.astype(jnp.int32)


def pack_kernel(devs, cap, authors, ends, out):
    auts, width = authors.shape
    edges = ends.shape[1]
    lines = out.shape[0]
    side = cap // HALVES
    position = edge_slots(ends[0:1, :], devs, cap)
    author_edge = where_equal(iota((auts, edges), 0), ends[1:2, :])
    rows = ends[2:3, :] + 1
    lane = iota((AUX, edges), 0)
    line = iota((lines, edges), 0) * side
    picked, aux = [], jnp.zeros((lines, AUX), F32)
    for q in range(side):
        slot_edge = where_equal(line + q, position)
        picked.append(mm(slot_edge, author_edge, NT).astype(BF))
        aux = aux + mm(slot_edge, jnp.where(lane == q, rows, 0).astype(F32).astype(BF), NT)
    out[:, side * width :] = aux.astype(BF)
    for q in range(side):
        out[:, q * width : (q + 1) * width] = mm(picked[q], authors[...], NN).astype(BF)


def base_kernel(devs, cap, papers, low, high, cite, w_self, w_cite, bias, ends, base, owner):
    rows = papers.shape[0]
    ext = rows + 2 * RIM
    column = iota((ext, rows), 0)
    picks = jnp.zeros((ext, rows), F32)
    for which in range(K_CIT):
        picks = picks + (column == cite[which : which + 1, :]).astype(F32)
    picks = picks.astype(BF)
    cites = mm(picks[:RIM], low[...], TN)
    cites = cites + mm(picks[RIM : RIM + rows], papers[...], TN)
    cites = cites + mm(picks[RIM + rows :], high[...], TN)
    cite_agg = (cites * (1.0 / K_CIT)).astype(BF)
    pre = mm(papers[...], w_self[...], NN)
    base[...] = pre + mm(cite_agg, w_cite[...], NN) + bias[...]
    total, auts = owner.shape
    edges = ends.shape[1]
    slot_edge = where_equal(iota((total, edges), 0), edge_slots(ends[0:1, :], devs, cap))
    author_edge = where_equal(iota((auts, edges), 0), ends[1:2, :])
    owner[...] = mm(slot_edge, author_edge, NT).astype(BF)


def split_match(arrived, width, rows):
    lines = arrived.shape[0]
    side = (arrived.shape[1] - AUX) // width
    aux = arrived[:, side * width :].astype(F32)
    wanted = iota((lines, rows), 1).astype(F32) + 1.0
    match = [where_equal(aux[:, q : q + 1], wanted) for q in range(side)]
    return jnp.concatenate(match, axis=0), aux


def side_rows(arrived, width):
    side = (arrived.shape[1] - AUX) // width
    return jnp.concatenate(
        [arrived[:, q * width : (q + 1) * width] for q in range(side)], axis=0
    )


def node_kernel(arrived, base, cotangent, w_aut, updated, slot_grad, scaled_out):
    width = w_aut.shape[0]
    rows = base.shape[0]
    total = slot_grad.shape[0]
    lines = arrived.shape[0]
    side = total // lines
    match, aux = split_match(arrived, width, rows)
    messages = mm(side_rows(arrived, width), w_aut[...], NN).astype(BF)
    aut_sum = mm(match, messages, TN)
    count = mm(match, jnp.ones((total, AUX), BF), TN)[:, :1]
    inverse = 1.0 / jnp.maximum(count, 1.0)
    pre = base[...] + aut_sum * inverse
    sigma = jax.nn.sigmoid(pre)
    updated[...] = (pre * sigma).astype(BF)
    delta = cotangent[...].astype(F32) * sigma * (1.0 + pre * (1.0 - sigma))
    scaled = (delta * inverse).astype(BF)
    scaled_out[...] = scaled
    spread = where_equal(iota((total, lines), 0) // side, iota((total, lines), 1))
    lanes = mm(spread, aux.astype(BF), NN)
    own_lane = iota((total, AUX), 1) == iota((total, AUX), 0) % side
    row_of = jnp.sum(jnp.where(own_lane, lanes, 0.0), axis=1, keepdims=True)
    slot_match = where_equal(row_of, iota((total, rows), 1).astype(F32) + 1.0)
    slot_grad[...] = mm(slot_match, scaled, NN).astype(BF)


def weight_kernel(arrived, scaled, partial):
    width = partial.shape[0]
    match, _ = split_match(arrived, width, scaled.shape[0])
    grads = mm(match, scaled[...], NN).astype(BF)
    partial[...] = mm(side_rows(arrived, width), grads, TN).astype(BF)


def author_kernel(returned, owner, w_aut, grad_authors):
    grad_proj = mm(owner[...], returned[...], TN).astype(BF)
    grad_authors[...] = mm(grad_proj, w_aut[...], NT).astype(BF)


def spread_kernel(scale, side, blocks, out):
    count, rows, lanes = blocks.shape
    near = count // (side * side)
    halves = near // 2
    for n in range(count):
        group, place = n // near, n % near
        core, z = place % 2, place // 2
        at = (core * side * side + group) * rows
        column = 0
        for bit in range(halves.bit_length() - 1):
            column = column * 2 + (z >> bit & 1)
        out[at : at + rows, column * lanes : (column + 1) * lanes] = blocks[n].astype(F32) * scale


def shift_sum(block, place, count, axis, perm):
    size = block.shape[0] // count

    def piece(at):
        return lax.dynamic_slice(
            block, (at * size, 0), (size, block.shape[1]), allow_negative_indices=False
        )

    came = [
        lax.ppermute(piece(lax.rem(place + k, count)), axis, perm(k)) for k in range(1, count)
    ]
    total = piece(place).astype(F32)
    for other in came:
        total = total + other.astype(F32)
    return total


def half_sum(block, bit, axis, perm):
    size = block.shape[1] // 2

    def piece(at):
        return lax.dynamic_slice(
            block, (0, at * size), (block.shape[0], size), allow_negative_indices=False
        )

    came = lax.ppermute(piece(1 - bit), axis, perm)
    return piece(bit).astype(F32) + came.astype(F32)


def reduce_weight(partial, grp_count, dev_count):
    side = math.isqrt(grp_count)
    grp = lax.axis_index("grp")
    dev = lax.axis_index("dev")
    x, y = lax.div(grp, side), lax.rem(grp, side)

    def along_x(k):
        return [(g, (g // side + k) % side * side + g % side) for g in range(grp_count)]

    def along_y(k):
        return [(g, g // side * side + (g % side + k) % side) for g in range(grp_count)]

    def along_dev(k):
        return [(d, d ^ k) for d in range(dev_count)]

    part = shift_sum(partial, dev & 1, 2, "dev", lambda k: along_dev(k)).astype(BF)
    part = shift_sum(part, x, side, "grp", along_x).astype(BF)
    part = shift_sum(part, y, side, "grp", along_y)
    step = 2
    while step < 2 * NEAR:
        part = half_sum(part, jnp.where(dev & step, 1, 0), "dev", along_dev(step))
        step = step * 2
    far = [list(range(i, dev_count, step)) for i in range(step)]
    part = jnp.sum(lax.all_gather(part, "dev", axis_index_groups=far, axis=0), axis=0)
    return part.astype(BF)


def gather_weight(part, grp_count, dev_count, scale):
    near = 2 * NEAR
    rows, lanes = part.shape
    groups = [[b * near + i for i in range(near)] for b in range(dev_count // near)]
    part = lax.all_to_all(
        jnp.broadcast_to(part[None], (near, rows, lanes)),
        "dev",
        0,
        0,
        axis_index_groups=groups,
        tiled=True,
    )
    blocks = lax.all_to_all(
        jnp.broadcast_to(part[None], (grp_count, near, rows, lanes)), "grp", 0, 0, tiled=True
    ).reshape(grp_count * near, rows, lanes)
    side = math.isqrt(grp_count)
    shape = jax.ShapeDtypeStruct((2 * grp_count * rows, NEAR * lanes), F32)
    (whole,) = call(functools.partial(spread_kernel, scale, side), (shape,), (blocks,), 0)
    return whole


def per_device(
    papers,
    authors,
    cotangent,
    w_self,
    w_cite,
    w_aut,
    bias,
    cite_col,
    edge_author,
    edge_dest,
    edge_row,
):
    dev_count = lax.axis_size("dev")
    grp_count = lax.axis_size("grp")
    pap_rows, width = papers.shape
    aut_rows = authors.shape[0]
    edges = edge_author.shape[0]
    slots = 2 * edges // dev_count
    total = dev_count * slots
    hidden = w_aut.shape[1]
    lines = dev_count * HALVES
    line = slots // HALVES * width + AUX
    shape = jax.ShapeDtypeStruct
    ends = jnp.stack([edge_dest[:, 0], edge_author, edge_row])

    (outgoing,) = call(
        functools.partial(pack_kernel, dev_count, slots),
        (shape((lines, line), BF),),
        (authors, ends),
        2 * total * aut_rows * (edges + width),
    )
    arrived = lax.all_to_all(
        outgoing.reshape(dev_count, HALVES, line), "dev", 0, 0, tiled=True
    ).reshape(lines, line)
    forward = [(i, i + 1) for i in range(dev_count - 1)]
    backward = [(i + 1, i) for i in range(dev_count - 1)]
    low = lax.ppermute(papers[pap_rows - RIM :], "dev", forward)
    high = lax.ppermute(papers[:RIM], "dev", backward)
    base, owner = call(
        functools.partial(base_kernel, dev_count, slots),
        (shape((pap_rows, hidden), F32), shape((total, aut_rows), BF)),
        (papers, low, high, cite_col.T, w_self, w_cite, bias.reshape(1, hidden), ends),
        2 * pap_rows * width * (2 * hidden + pap_rows + 2 * RIM),
    )
    updated, slot_grad, scaled = call(
        node_kernel,
        (
            shape((pap_rows, hidden), BF),
            shape((total, hidden), BF),
            shape((pap_rows, hidden), BF),
        ),
        (arrived, base, cotangent, w_aut),
        2 * total * hidden * (width + 2 * pap_rows),
    )
    returned = lax.all_to_all(
        slot_grad.reshape(dev_count, slots, hidden), "dev", 0, 0, tiled=True
    ).reshape(total, hidden)
    (partial,) = call(
        weight_kernel,
        (shape((width, hidden), BF),),
        (arrived, scaled),
        2 * total * width * hidden,
    )
    part = reduce_weight(partial, grp_count, dev_count)
    part, returned = lax.optimization_barrier((part, returned))
    (grad_authors,) = call(
        author_kernel,
        (shape((aut_rows, width), BF),),
        (returned, owner, w_aut),
        2 * aut_rows * hidden * (total + width),
    )
    scale = 1.0 / math.sqrt(grp_count * dev_count * aut_rows)
    grad_w_aut = gather_weight(part, grp_count, dev_count, scale)
    return (updated, grad_authors, grad_w_aut)


def solution(mesh):
    placed = (
        P(("grp", "dev"), None),
        P(("grp", "dev"), None),
        P(("grp", "dev"), None),
        P(),
        P(),
        P(),
        P(),
        P(("grp", "dev"), None),
        P(("grp", "dev")),
        P(("grp", "dev"), None),
        P(("grp", "dev")),
    )
    return jax.shard_map(
        per_device,
        mesh=mesh,
        in_specs=placed,
        out_specs=(P(("grp", "dev"), None), P(("grp", "dev"), None), P()),
        check_vma=False,
    )
```

time: 281 us -> 266 us (0.947); the launches traced: 277 us -> 265 us
  blocking collectives: 79.3 us -> 58.2 us
  waiting for transfers between devices: 102 us -> 110 us
    all_gather x3 -> x1, blocking collectives: 79.3 us -> 42.7 us  [reduce_weight(): lax.all_gather(part, 'dev', axis_index_groups=far, axis=0)]
    all_to_all x0 -> x1, blocking collectives: none -> 15.5 us  [gather_weight(): lax.all_to_all(jnp.broadcast_to(part[None], (near, rows, lanes)), 'dev',...]
    ppermute x10 -> x7, starting transfers between devices: 34.7 us -> 22.4 us  [shift_sum(): lax.ppermute(piece(lax.rem(place + k, count)), axis, perm(k))]
    all_to_all x1 -> x2, waiting for transfers between devices: 15.7 us -> 27 us  [the longest x1 15.7 us: per_device(): lax.all_to_all(outgoing.reshape(dev_count, HALVES, line), 'dev', 0, 0, ti...]
    ppermute x0 -> x2, waiting for transfers between devices: none -> 9.78 us  [half_sum(): came = lax.ppermute(piece(1 - bit), axis, perm)]
    ppermute x1, waiting for transfers between devices: 73.7 us -> 65.5 us  [per_device(): high = lax.ppermute(papers[:RIM], 'dev', backward)]
    ppermute x0 -> x2, starting transfers between devices: none -> 7.16 us  [half_sum(): came = lax.ppermute(piece(1 - bit), axis, perm)]
    all_to_all x1 -> x2, starting transfers between devices: 30.4 us -> 37.3 us  [the longest x1 30.6 us: per_device(): lax.all_to_all(outgoing.reshape(dev_count, HALVES, line), 'dev', 0, 0, ti...]
  transfers between devices with their start and end apart: 14 -> 14, of which waited for: 7 -> 8; matrix products, arithmetic and copies ran while one was open for 1% -> 0% of each run, Pallas kernels for 1% -> 1%
where the time goes in v2:
time: 266 us; the launch traced here: 265 us
  waiting for transfers between devices  110 us (41%)
  starting transfers between devices  80.5 us (30%)
  blocking collectives  58.2 us (22%)
  Pallas kernels  7.88 us (3%)
  local copies, waits for them, and re-layouts  6.6 us (2%)
    ppermute x1, waiting for transfers between devices, per_device(): high = lax.ppermute(papers[:RIM], 'dev', backward)  65.5 us
    all_gather x1, blocking collectives, reduce_weight(): lax.all_gather(part, 'dev', axis_index_groups=far, axis=0)  42.7 us
    all_to_all x1, starting transfers between devices, per_device(): lax.all_to_all(outgoing.reshape(dev_count, HALVES, line), 'dev', 0, 0, ti...  30.6 us
    ppermute x7, starting transfers between devices, shift_sum(): lax.ppermute(piece(lax.rem(place + k, count)), axis, perm(k))  22.4 us
    all_to_all x1, waiting for transfers between devices, per_device(): lax.all_to_all(outgoing.reshape(dev_count, HALVES, line), 'dev', 0, 0, ti...  15.7 us
    all_to_all x1, blocking collectives, gather_weight(): lax.all_to_all(jnp.broadcast_to(part[None], (near, rows, lanes)), 'dev',...  15.5 us
    all_to_all x1, waiting for transfers between devices, gather_weight(): lax.all_to_all(jnp.broadcast_to(part[None], (grp_count, near, rows, lanes...  11.4 us
    ppermute x2, waiting for transfers between devices, half_sum(): came = lax.ppermute(piece(1 - bit), axis, perm)  9.78 us
  transfers between devices with their start and end apart: 14, of which 8 were waited for; matrix products, arithmetic and copies ran while one was open for 0% of the time, Pallas kernels for 1%

profile of v2, /device:TPU:1, one launch (start us, length us, event | category | flops | bytes accessed | tf_op | source)
XLA Modules:
  0.0 265.2 jit_solution(861816600011114596)
XLA Ops:
  1.4 1.0 copy-done.4
  3.1 1.2 reshape.26
  4.3 30.6 %all-to-all-start = ((bf16[64,2,3200]{2,1,0:T(2,128)(2,1)}), bf16[64,2,3200]{2,1,0:T(2,128)(2,1)}, u32[]{:S(2)}, u32[]{:S(2)}) async-start(bf16[64,2,3200]{2,1,0:T(2,128)(2,1)} %reshape.26), calls=%async_computation | async-start | bytes 1638400 | tf_op jit(solution)/shard_map/all_to_all | solution.py:271
  34.9 2.4 collective-permute-start.1
  37.4 3.1 %collective-permute-start = (bf16[64,768]{1,0:T(8,128)(2,1)S(1)}, bf16[64,768]{1,0:T(8,128)(2,1)S(1)}, u32[]{:S(2)}, u32[]{:S(2)}) collective-permute-start(bf16[64,768]{1,0:T(8,128)(2,1)S(1)} %get-tuple-element.21), channel_id=1, source_target_pairs={{0,1},{1,2},{2,3},{3,4},{4,5},{5,6},{6,7},{7,8},{8,9},{9,10},{10,1... | collective-permute-start | bytes 294920 | tf_op jit(solution)/shard_map/ppermute | solution.py:276
  40.5 65.5 %collective-permute-done.1.high = bf16[64,768]{1,0:T(8,128)(2,1)S(1)} collective-permute-done((bf16[64,768]{1,0:T(8,128)(2,1)S(1)}, bf16[64,768]{1,0:T(8,128)(2,1)S(1)}, u32[]{:S(2)}, u32[]{:S(2)}) %collective-permute-start.1) | collective-permute-done | bytes 98336 | tf_op jit(solution)/shard_map/ppermute | solution.py:277
  106.0 1.4 shard_map.131
  108.3 15.7 %all-to-all-done = bf16[64,2,3200]{2,1,0:T(2,128)(2,1)} async-done(((bf16[64,2,3200]{2,1,0:T(2,128)(2,1)}), bf16[64,2,3200]{2,1,0:T(2,128)(2,1)}, u32[]{:S(2)}, u32[]{:S(2)}) %all-to-all-start) | async-done | bytes 819232 | tf_op jit(solution)/shard_map/all_to_all | solution.py:271
  124.0 2.4 reshape.27.arrived
  126.4 2.3 shard_map.132
  128.7 8.0 %all-to-all-start.1 = ((bf16[64,8,512]{2,1,0:T(8,128)(2,1)}), bf16[64,8,512]{2,1,0:T(8,128)(2,1)S(1)}, u32[]{:S(2)}, u32[]{:S(2)}) async-start(bf16[64,8,512]{2,1,0:T(8,128)(2,1)} %bitcast.6), calls=%async_computation.1 | async-start | bytes 1048576 | tf_op jit(solution)/shard_map/all_to_all | solution.py:294
  137.6 2.4 collective-permute-start.2
  140.0 1.3 collective-permute-done.2
  141.5 3.1 %collective-permute-start.3 = (bf16[96,512]{1,0:T(8,128)(2,1)S(1)}, bf16[96,512]{1,0:T(8,128)(2,1)S(1)}, u32[]{:S(2)}, u32[]{:S(2)}) collective-permute-start(bf16[96,512]{1,0:T(8,128)(2,1)S(1)} %get-tuple-element.17), channel_id=1, source_target_pairs={{0,256},{64,320},{128,384},{192,448},{256,512},{320,576},{384,640}... | collective-permute-start | bytes 294920 | tf_op jit(solution)/shard_map/ppermute | solution.py:171
  144.6 3.4 %collective-permute-start.5 = (bf16[96,512]{1,0:T(8,128)(2,1)S(1)}, bf16[96,512]{1,0:T(8,128)(2,1)S(1)}, u32[]{:S(2)}, u32[]{:S(2)}) collective-permute-start(bf16[96,512]{1,0:T(8,128)(2,1)S(1)} %get-tuple-element.18), channel_id=1, source_target_pairs={{0,768},{64,832},{128,896},{192,960},{256,0},{320,64},{384,128},{4... | collective-permute-start | bytes 294920 | tf_op jit(solution)/shard_map/ppermute | solution.py:171
  148.0 3.4 %collective-permute-start.4 = (bf16[96,512]{1,0:T(8,128)(2,1)S(1)}, bf16[96,512]{1,0:T(8,128)(2,1)S(1)}, u32[]{:S(2)}, u32[]{:S(2)}) collective-permute-start(bf16[96,512]{1,0:T(8,128)(2,1)S(1)} %get-tuple-element.19), channel_id=1, source_target_pairs={{0,512},{64,576},{128,640},{192,704},{256,768},{320,832},{384,896}... | collective-permute-start | bytes 294920 | tf_op jit(solution)/shard_map/ppermute | solution.py:171
  151.5 3.7 %collective-permute-done.4 = bf16[96,512]{1,0:T(8,128)(2,1)S(1)} collective-permute-done((bf16[96,512]{1,0:T(8,128)(2,1)S(1)}, bf16[96,512]{1,0:T(8,128)(2,1)S(1)}, u32[]{:S(2)}, u32[]{:S(2)}) %collective-permute-start.4) | collective-permute-done | bytes 98336 | tf_op jit(solution)/shard_map/ppermute | solution.py:171
  155.2 3.2 %collective-permute-start.6 = (bf16[24,512]{1,0:T(8,128)(2,1)S(1)}, bf16[24,512]{1,0:T(8,128)(2,1)S(1)}, u32[]{:S(2)}, u32[]{:S(2)}) collective-permute-start(bf16[24,512]{1,0:T(8,128)(2,1)S(1)} %get-tuple-element.22), channel_id=1, source_target_pairs={{0,64},{64,128},{128,192},{192,0},{256,320},{320,384},{384,448},{4... | collective-permute-start | bytes 73736 | tf_op jit(solution)/shard_map/ppermute | solution.py:171
  158.4 3.4 %collective-permute-start.8 = (bf16[24,512]{1,0:T(8,128)(2,1)S(1)}, bf16[24,512]{1,0:T(8,128)(2,1)S(1)}, u32[]{:S(2)}, u32[]{:S(2)}) collective-permute-start(bf16[24,512]{1,0:T(8,128)(2,1)S(1)} %get-tuple-element.23), channel_id=1, source_target_pairs={{0,192},{64,0},{128,64},{192,128},{256,448},{320,256},{384,320},{4... | collective-permute-start | bytes 73736 | tf_op jit(solution)/shard_map/ppermute | solution.py:171
  161.8 3.5 %collective-permute-start.7 = (bf16[24,512]{1,0:T(8,128)(2,1)S(1)}, bf16[24,512]{1,0:T(8,128)(2,1)S(1)}, u32[]{:S(2)}, u32[]{:S(2)}) collective-permute-start(bf16[24,512]{1,0:T(8,128)(2,1)S(1)} %get-tuple-element.24), channel_id=1, source_target_pairs={{0,128},{64,192},{128,0},{192,64},{256,384},{320,448},{384,256},{4... | collective-permute-start | bytes 73736 | tf_op jit(solution)/shard_map/ppermute | solution.py:171
  165.4 2.8 %collective-permute-done.7 = bf16[24,512]{1,0:T(8,128)(2,1)S(1)} collective-permute-done((bf16[24,512]{1,0:T(8,128)(2,1)S(1)}, bf16[24,512]{1,0:T(8,128)(2,1)S(1)}, u32[]{:S(2)}, u32[]{:S(2)}) %collective-permute-start.7) | collective-permute-done | bytes 24608 | tf_op jit(solution)/shard_map/ppermute | solution.py:171
  168.2 3.2 %collective-permute-start.9 = (f32[24,256]{1,0:T(8,128)S(1)}, f32[24,256]{1,0:T(8,128)S(1)}, u32[]{:S(2)}, u32[]{:S(2)}) collective-permute-start(f32[24,256]{1,0:T(8,128)S(1)} %constant_dynamic-slice_fusion.1), channel_id=1, source_target_pairs={{0,2},{1,3},{2,0},{3,1},{4,6},{5,7},{6,4},{7,5},{8,10},{9,11},{10,... | collective-permute-start | bytes 73736 | tf_op jit(solution)/shard_map/ppermute | solution.py:187
  171.4 8.0 %collective-permute-done.9 = f32[24,256]{1,0:T(8,128)S(1)} collective-permute-done((f32[24,256]{1,0:T(8,128)S(1)}, f32[24,256]{1,0:T(8,128)S(1)}, u32[]{:S(2)}, u32[]{:S(2)}) %collective-permute-start.9) | collective-permute-done | bytes 24608 | tf_op jit(solution)/shard_map/ppermute | solution.py:187
  179.5 3.9 %collective-permute-start.10 = (f32[24,128]{1,0:T(8,128)S(1)}, f32[24,128]{1,0:T(8,128)S(1)}, u32[]{:S(2)}, u32[]{:S(2)}) collective-permute-start(f32[24,128]{1,0:T(8,128)S(1)} %constant_dynamic-slice_fusion), channel_id=1, source_target_pairs={{0,4},{1,5},{2,6},{3,7},{4,0},{5,1},{6,2},{7,3},{8,12},{9,13},{10,... | collective-permute-start | bytes 36872 | tf_op jit(solution)/shard_map/ppermute | solution.py:187
  183.4 1.8 collective-permute-done.10
  185.2 42.7 %all-gather = f32[192,128]{1,0:T(8,128)S(1)} all-gather(f32[24,128]{1,0:T(8,128)S(1)} %dynamic-slice_add_fusion.1), channel_id=2, replica_groups={{0,8,16,24,32,40,48,56},{1,9,17,25,33,41,49,57},{2,10,18,26,34,42,50,58..., dimensions={0}, use_global_device_ids=true | all-gather | bytes 110592 | tf_op jit(solution)/shard_map/all_gather | solution.py:214
  228.0 15.5 %all_to_all.20 = bf16[8,24,128]{2,1,0:T(8,128)(2,1)S(1)} all-to-all(bf16[8,24,128]{2,1,0:T(8,128)(2,1)S(1)} %broadcast_in_dim.4), channel_id=1, replica_groups={{0,1,2,3,4,5,6,7},{8,9,10,11,12,13,14,15},{16,17,18,19,20,21,22,23},{24..., dimensions={0} | all-to-all | bytes 98304 | tf_op jit(solution)/shard_map/all_to_all | solution.py:222
  243.4 1.0 broadcast_in_dim.5
  244.5 6.8 %all-to-all-start.3 = ((bf16[16,8,24,128]{3,2,1,0:T(8,128)(2,1)}), bf16[16,8,24,128]{3,2,1,0:T(8,128)(2,1)S(1)}, u32[]{:S(2)}, u32[]{:S(2)}) async-start(bf16[16,8,24,128]{3,2,1,0:T(8,128)(2,1)} %broadcast_in_dim.5), calls=%async_computation.3 | async-start | bytes 1572864 | tf_op jit(solution)/shard_map/all_to_all | solution.py:230
  251.2 1.4 shard_map.134
  252.6 11.4 %all-to-all-done.3 = bf16[16,8,24,128]{3,2,1,0:T(8,128)(2,1)S(1)} async-done(((bf16[16,8,24,128]{3,2,1,0:T(8,128)(2,1)}), bf16[16,8,24,128]{3,2,1,0:T(8,128)(2,1)S(1)}, u32[]{:S(2)}, u32[]{:S(2)}) %all-to-all-start.3) | async-done | bytes 786464 | tf_op jit(solution)/shard_map/all_to_all | solution.py:230
  264.0 1.2 shard_map.135
  (41 shorter events, 3.5 us)
Async XLA Ops:
  1.4 1.0 copy-start.4
  3.1 31.8 %copy-start = (bf16[256,768]{1,0:T(8,128)(2,1)S(1)}, bf16[256,768]{1,0:T(8,128)(2,1)}, u32[]{:S(2)}) copy-start(bf16[256,768]{1,0:T(8,128)(2,1)} %papers.1) | copy-start | bytes 1179652
  3.1 102.9 %copy-start.1 = (bf16[768,512]{1,0:T(8,128)(2,1)S(1)}, bf16[768,512]{1,0:T(8,128)(2,1)}, u32[]{:S(2)}) copy-start(bf16[768,512]{1,0:T(8,128)(2,1)} %w_self.1) | copy-start | bytes 2359300
  3.1 102.9 %copy-start.2 = (bf16[768,512]{1,0:T(8,128)(2,1)S(1)}, bf16[768,512]{1,0:T(8,128)(2,1)}, u32[]{:S(2)}) copy-start(bf16[768,512]{1,0:T(8,128)(2,1)} %w_cite.1) | copy-start | bytes 2359300
  3.1 102.9 %copy-start.5 = (s32[256,8]{0,1:T(8,128)S(1)}, s32[256,8]{0,1:T(8,128)}, u32[]{:S(2)}) copy-start(s32[256,8]{0,1:T(8,128)} %param.18) | copy-start | bytes 24580
  3.1 102.9 %copy-start.6 = (f32[512]{0:T(512)S(1)}, f32[512]{0:T(512)}, u32[]{:S(2)}) copy-start(f32[512]{0:T(512)} %param.17) | copy-start | bytes 6148
  4.3 119.7 %all-to-all-start = ((bf16[64,2,3200]{2,1,0:T(2,128)(2,1)}), bf16[64,2,3200]{2,1,0:T(2,128)(2,1)}, u32[]{:S(2)}, u32[]{:S(2)}) async-start(bf16[64,2,3200]{2,1,0:T(2,128)(2,1)} %reshape.26), calls=%async_computation | async-start | bytes 1638400 | tf_op jit(solution)/shard_map/all_to_all | solution.py:271
  34.9 71.1 %collective-permute-start.1 = (bf16[64,768]{1,0:T(8,128)(2,1)S(1)}, bf16[64,768]{1,0:T(8,128)(2,1)S(1)}, u32[]{:S(2)}, u32[]{:S(2)}) collective-permute-start(bf16[64,768]{1,0:T(8,128)(2,1)S(1)} %get-tuple-element.20), channel_id=1, source_target_pairs={{1,0},{2,1},{3,2},{4,3},{5,4},{6,5},{7,6},{8,7},{9,8},{10,9},{11,1... | collective-permute-start | bytes 294920 | tf_op jit(solution)/shard_map/ppermute | solution.py:277
  37.4 68.6 %collective-permute-start = (bf16[64,768]{1,0:T(8,128)(2,1)S(1)}, bf16[64,768]{1,0:T(8,128)(2,1)S(1)}, u32[]{:S(2)}, u32[]{:S(2)}) collective-permute-start(bf16[64,768]{1,0:T(8,128)(2,1)S(1)} %get-tuple-element.21), channel_id=1, source_target_pairs={{0,1},{1,2},{2,3},{3,4},{4,5},{5,6},{6,7},{7,8},{8,9},{9,10},{10,1... | collective-permute-start | bytes 294920 | tf_op jit(solution)/shard_map/ppermute | solution.py:276
  107.5 0.8 copy-start.7
  108.3 18.1 %copy-start.3 = (bf16[768,512]{1,0:T(8,128)(2,1)S(1)}, bf16[768,512]{1,0:T(8,128)(2,1)}, u32[]{:S(2)}) copy-start(bf16[768,512]{1,0:T(8,128)(2,1)} %w_aut.3) | copy-start | bytes 2359300
  108.3 18.1 %copy-start.9 = (bf16[256,512]{1,0:T(8,128)(2,1)S(1)}, bf16[256,512]{1,0:T(8,128)(2,1)}, u32[]{:S(2)}) copy-start(bf16[256,512]{1,0:T(8,128)(2,1)} %cotangent.1) | copy-start | bytes 786436
  124.0 2.4 copy-start.8
  128.7 99.3 %all-to-all-start.1 = ((bf16[64,8,512]{2,1,0:T(8,128)(2,1)}), bf16[64,8,512]{2,1,0:T(8,128)(2,1)S(1)}, u32[]{:S(2)}, u32[]{:S(2)}) async-start(bf16[64,8,512]{2,1,0:T(8,128)(2,1)} %bitcast.6), calls=%async_computation.1 | async-start | bytes 1048576 | tf_op jit(solution)/shard_map/all_to_all | solution.py:294
  137.6 3.7 %collective-permute-start.2 = (bf16[384,512]{1,0:T(8,128)(2,1)S(1)}, bf16[384,512]{1,0:T(8,128)(2,1)S(1)}, u32[]{:S(2)}, u32[]{:S(2)}) collective-permute-start(bf16[384,512]{1,0:T(8,128)(2,1)S(1)} %constant_dynamic-slice_fusion.8), channel_id=1, source_target_pairs={{0,1},{1,0},{2,3},{3,2},{4,5},{5,4},{6,7},{7,6},{8,9},{9,8},{10,11... | collective-permute-start | bytes 1179656 | tf_op jit(solution)/shard_map/ppermute | solution.py:171
  141.5 10.0 %collective-permute-start.3 = (bf16[96,512]{1,0:T(8,128)(2,1)S(1)}, bf16[96,512]{1,0:T(8,128)(2,1)S(1)}, u32[]{:S(2)}, u32[]{:S(2)}) collective-permute-start(bf16[96,512]{1,0:T(8,128)(2,1)S(1)} %get-tuple-element.17), channel_id=1, source_target_pairs={{0,256},{64,320},{128,384},{192,448},{256,512},{320,576},{384,640}... | collective-permute-start | bytes 294920 | tf_op jit(solution)/shard_map/ppermute | solution.py:171
  144.6 6.9 %collective-permute-start.5 = (bf16[96,512]{1,0:T(8,128)(2,1)S(1)}, bf16[96,512]{1,0:T(8,128)(2,1)S(1)}, u32[]{:S(2)}, u32[]{:S(2)}) collective-permute-start(bf16[96,512]{1,0:T(8,128)(2,1)S(1)} %get-tuple-element.18), channel_id=1, source_target_pairs={{0,768},{64,832},{128,896},{192,960},{256,0},{320,64},{384,128},{4... | collective-permute-start | bytes 294920 | tf_op jit(solution)/shard_map/ppermute | solution.py:171
  148.0 7.2 %collective-permute-start.4 = (bf16[96,512]{1,0:T(8,128)(2,1)S(1)}, bf16[96,512]{1,0:T(8,128)(2,1)S(1)}, u32[]{:S(2)}, u32[]{:S(2)}) collective-permute-start(bf16[96,512]{1,0:T(8,128)(2,1)S(1)} %get-tuple-element.19), channel_id=1, source_target_pairs={{0,512},{64,576},{128,640},{192,704},{256,768},{320,832},{384,896}... | collective-permute-start | bytes 294920 | tf_op jit(solution)/shard_map/ppermute | solution.py:171
  155.2 10.1 %collective-permute-start.6 = (bf16[24,512]{1,0:T(8,128)(2,1)S(1)}, bf16[24,512]{1,0:T(8,128)(2,1)S(1)}, u32[]{:S(2)}, u32[]{:S(2)}) collective-permute-start(bf16[24,512]{1,0:T(8,128)(2,1)S(1)} %get-tuple-element.22), channel_id=1, source_target_pairs={{0,64},{64,128},{128,192},{192,0},{256,320},{320,384},{384,448},{4... | collective-permute-start | bytes 73736 | tf_op jit(solution)/shard_map/ppermute | solution.py:171
  158.4 6.9 %collective-permute-start.8 = (bf16[24,512]{1,0:T(8,128)(2,1)S(1)}, bf16[24,512]{1,0:T(8,128)(2,1)S(1)}, u32[]{:S(2)}, u32[]{:S(2)}) collective-permute-start(bf16[24,512]{1,0:T(8,128)(2,1)S(1)} %get-tuple-element.23), channel_id=1, source_target_pairs={{0,192},{64,0},{128,64},{192,128},{256,448},{320,256},{384,320},{4... | collective-permute-start | bytes 73736 | tf_op jit(solution)/shard_map/ppermute | solution.py:171
  161.8 6.4 %collective-permute-start.7 = (bf16[24,512]{1,0:T(8,128)(2,1)S(1)}, bf16[24,512]{1,0:T(8,128)(2,1)S(1)}, u32[]{:S(2)}, u32[]{:S(2)}) collective-permute-start(bf16[24,512]{1,0:T(8,128)(2,1)S(1)} %get-tuple-element.24), channel_id=1, source_target_pairs={{0,128},{64,192},{128,0},{192,64},{256,384},{320,448},{384,256},{4... | collective-permute-start | bytes 73736 | tf_op jit(solution)/shard_map/ppermute | solution.py:171
  168.2 11.2 %collective-permute-start.9 = (f32[24,256]{1,0:T(8,128)S(1)}, f32[24,256]{1,0:T(8,128)S(1)}, u32[]{:S(2)}, u32[]{:S(2)}) collective-permute-start(f32[24,256]{1,0:T(8,128)S(1)} %constant_dynamic-slice_fusion.1), channel_id=1, source_target_pairs={{0,2},{1,3},{2,0},{3,1},{4,6},{5,7},{6,4},{7,5},{8,10},{9,11},{10,... | collective-permute-start | bytes 73736 | tf_op jit(solution)/shard_map/ppermute | solution.py:187
  179.5 5.7 %collective-permute-start.10 = (f32[24,128]{1,0:T(8,128)S(1)}, f32[24,128]{1,0:T(8,128)S(1)}, u32[]{:S(2)}, u32[]{:S(2)}) collective-permute-start(f32[24,128]{1,0:T(8,128)S(1)} %constant_dynamic-slice_fusion), channel_id=1, source_target_pairs={{0,4},{1,5},{2,6},{3,7},{4,0},{5,1},{6,2},{7,3},{8,12},{9,13},{10,... | collective-permute-start | bytes 36872 | tf_op jit(solution)/shard_map/ppermute | solution.py:187
  244.5 19.5 %all-to-all-start.3 = ((bf16[16,8,24,128]{3,2,1,0:T(8,128)(2,1)}), bf16[16,8,24,128]{3,2,1,0:T(8,128)(2,1)S(1)}, u32[]{:S(2)}, u32[]{:S(2)}) async-start(bf16[16,8,24,128]{3,2,1,0:T(8,128)(2,1)} %broadcast_in_dim.5), calls=%async_computation.3 | async-start | bytes 1572864 | tf_op jit(solution)/shard_map/all_to_all | solution.py:230

commit v3 on v2

--- a/solution.py
+++ b/solution.py
@@ -12,7 +12,6 @@
 K_CIT = 8
 AUX = 128
 HALVES = 2
-NEAR = 4
 BF = jnp.bfloat16
 F32 = jnp.float32
 NN = (((1,), (0,)), ((), ()))
@@ -145,18 +144,21 @@
     grad_authors[...] = mm(grad_proj, w_aut[...], NT).astype(BF)
 
 
-def spread_kernel(scale, side, blocks, out):
-    count, rows, lanes = blocks.shape
-    near = count // (side * side)
-    halves = near // 2
-    for n in range(count):
-        group, place = n // near, n % near
-        core, z = place % 2, place // 2
-        at = (core * side * side + group) * rows
-        column = 0
-        for bit in range(halves.bit_length() - 1):
-            column = column * 2 + (z >> bit & 1)
-        out[at : at + rows, column * lanes : (column + 1) * lanes] = blocks[n].astype(F32) * scale
+def ring_kernel(every, out):
+    total = every[0].astype(F32)
+    for n in range(1, every.shape[0]):
+        total = total + every[n].astype(F32)
+    total = total.astype(BF)
+    for n in range(out.shape[0]):
+        out[n] = total
+
+
+def spread_kernel(scale, own, other, core, out):
+    half = own.shape[0]
+    first = core[0] == 0
+    mine, came = own[...].astype(F32) * scale, other[...].astype(F32) * scale
+    out[:half, :] = jnp.where(first, mine, came)
+    out[half:, :] = jnp.where(first, came, mine)
 
 
 def shift_sum(block, place, count, axis, perm):
@@ -176,22 +178,14 @@
     return total
 
 
-def half_sum(block, bit, axis, perm):
-    size = block.shape[1] // 2
-
-    def piece(at):
-        return lax.dynamic_slice(
-            block, (0, at * size), (block.shape[0], size), allow_negative_indices=False
-        )
-
-    came = lax.ppermute(piece(1 - bit), axis, perm)
-    return piece(bit).astype(F32) + came.astype(F32)
+def swap(block):
+    return lax.ppermute(block, "dev", [(d, d ^ 1) for d in range(lax.axis_size("dev"))])
 
 
 def reduce_weight(partial, grp_count, dev_count):
     side = math.isqrt(grp_count)
     grp = lax.axis_index("grp")
-    dev = lax.axis_index("dev")
+    core = lax.axis_index("dev") & 1
     x, y = lax.div(grp, side), lax.rem(grp, side)
 
     def along_x(k):
@@ -200,39 +194,34 @@
     def along_y(k):
         return [(g, g // side * side + (g % side + k) % side) for g in range(grp_count)]
 
-    def along_dev(k):
+    def along_core(k):
         return [(d, d ^ k) for d in range(dev_count)]
 
-    part = shift_sum(partial, dev & 1, 2, "dev", lambda k: along_dev(k)).astype(BF)
+    part = shift_sum(partial, core, 2, "dev", along_core).astype(BF)
     part = shift_sum(part, x, side, "grp", along_x).astype(BF)
-    part = shift_sum(part, y, side, "grp", along_y)
-    step = 2
-    while step < 2 * NEAR:
-        part = half_sum(part, jnp.where(dev & step, 1, 0), "dev", along_dev(step))
-        step = step * 2
-    far = [list(range(i, dev_count, step)) for i in range(step)]
-    part = jnp.sum(lax.all_gather(part, "dev", axis_index_groups=far, axis=0), axis=0)
-    return part.astype(BF)
-
-
-def gather_weight(part, grp_count, dev_count, scale):
-    near = 2 * NEAR
-    rows, lanes = part.shape
-    groups = [[b * near + i for i in range(near)] for b in range(dev_count // near)]
-    part = lax.all_to_all(
-        jnp.broadcast_to(part[None], (near, rows, lanes)),
-        "dev",
-        0,
-        0,
-        axis_index_groups=groups,
-        tiled=True,
-    )
-    blocks = lax.all_to_all(
-        jnp.broadcast_to(part[None], (grp_count, near, rows, lanes)), "grp", 0, 0, tiled=True
-    ).reshape(grp_count * near, rows, lanes)
-    side = math.isqrt(grp_count)
-    shape = jax.ShapeDtypeStruct((2 * grp_count * rows, NEAR * lanes), F32)
-    (whole,) = call(functools.partial(spread_kernel, scale, side), (shape,), (blocks,), 0)
+    part = shift_sum(part, y, side, "grp", along_y).astype(BF)
+    ring = [list(range(i, dev_count, 2)) for i in range(2)]
+    every = lax.all_gather(part, "dev", axis_index_groups=ring, axis=0)
+    copies = jax.ShapeDtypeStruct((grp_count, *part.shape), BF)
+    (out,) = call(ring_kernel, (copies,), (every,), 0)
+    return out
+
+
+def gather_weight(copies, scale):
+    grp_count, rows, lanes = copies.shape
+    own = lax.all_to_all(copies, "grp", 0, 0, tiled=True).reshape(grp_count * rows, lanes)
+    other = swap(own)
+    core = (lax.axis_index("dev") & 1).reshape(1)
+    whole = pl.pallas_call(
+        functools.partial(spread_kernel, scale),
+        out_shape=jax.ShapeDtypeStruct((2 * grp_count * rows, lanes), F32),
+        in_specs=[
+            pl.BlockSpec(memory_space=pltpu.VMEM),
+            pl.BlockSpec(memory_space=pltpu.VMEM),
+            pl.BlockSpec(memory_space=pltpu.SMEM),
+        ],
+        compiler_params=pltpu.CompilerParams(vmem_limit_bytes=16 * 1024 * 1024),
+    )(own, other, core)
     return whole
 
 
@@ -309,7 +298,7 @@
         2 * aut_rows * hidden * (total + width),
     )
     scale = 1.0 / math.sqrt(grp_count * dev_count * aut_rows)
-    grad_w_aut = gather_weight(part, grp_count, dev_count, scale)
+    grad_w_aut = gather_weight(part, scale)
     return (updated, grad_authors, grad_w_aut)
 
 

time: 266 us -> 261 us (0.981)
  waiting for transfers between devices: 110 us -> 88.9 us
  blocking collectives: 58.2 us -> 72.9 us
    all_gather x1, blocking collectives: 42.7 us -> 59.6 us  [reduce_weight(): every = lax.all_gather(part, 'dev', axis_index_groups=ring, axis=0)]
    all_to_all x1 -> x0, waiting for transfers between devices: 11.4 us -> none  [gather_weight(): lax.all_to_all(jnp.broadcast_to(part[None], (grp_count, near, rows, lanes...]
    ppermute x2 -> x1, waiting for transfers between devices: 9.78 us -> 0.01 us  [swap(): lax.ppermute(block, 'dev', [(d, d ^ 1) for d in range(lax.axis_size('dev'...]
    ppermute x2 -> x1, starting transfers between devices: 7.16 us -> 16 us  [swap(): lax.ppermute(block, 'dev', [(d, d ^ 1) for d in range(lax.axis_size('dev'...]
    all_to_all x1 -> x0, starting transfers between devices: 6.76 us -> none  [gather_weight(): lax.all_to_all(jnp.broadcast_to(part[None], (grp_count, near, rows, lanes...]
  transfers between devices with their start and end apart: 14 -> 12, of which waited for: 8 -> 5; matrix products, arithmetic and copies ran while one was open for 0% -> 0% of each run, Pallas kernels for 1% -> 1%
where the time goes in v3:
time: 261 us; the launch traced here: 260 us
  waiting for transfers between devices  88.9 us (34%)
  starting transfers between devices  82.5 us (32%)
  blocking collectives  72.9 us (28%)
  Pallas kernels  8.12 us (3%)
  local copies, waits for them, and re-layouts  5.54 us (2%)
    ppermute x1, waiting for transfers between devices, per_device(): high = lax.ppermute(papers[:RIM], 'dev', backward)  65.5 us
    all_gather x1, blocking collectives, reduce_weight(): every = lax.all_gather(part, 'dev', axis_index_groups=ring, axis=0)  59.6 us
    all_to_all x1, starting transfers between devices, per_device(): lax.all_to_all(outgoing.reshape(dev_count, HALVES, line), 'dev', 0, 0, ti...  30.6 us
    ppermute x7, starting transfers between devices, shift_sum(): lax.ppermute(piece(lax.rem(place + k, count)), axis, perm(k))  22.4 us
    ppermute x1, starting transfers between devices, swap(): lax.ppermute(block, 'dev', [(d, d ^ 1) for d in range(lax.axis_size('dev'...  16 us
    all_to_all x1, waiting for transfers between devices, per_device(): lax.all_to_all(outgoing.reshape(dev_count, HALVES, line), 'dev', 0, 0, ti...  15.7 us
    all_to_all x1, blocking collectives, gather_weight(): lax.all_to_all(copies, 'grp', 0, 0, tiled=True)  13.3 us
    all_to_all x1, starting transfers between devices, per_device(): lax.all_to_all(slot_grad.reshape(dev_count, slots, hidden), 'dev', 0, 0,...  8.05 us
  transfers between devices with their start and end apart: 12, of which 5 were waited for; matrix products, arithmetic and copies ran while one was open for 0% of the time, Pallas kernels for 1%

profile of v3, /device:TPU:1, one launch (start us, length us, event | category | flops | bytes accessed | tf_op | source)
XLA Modules:
  0.0 260.0 jit_solution(11612515126391481008)
XLA Ops:
  0.6 0.7 pad_add_fusion.ends
  1.4 1.0 copy-done.4
  2.3 0.7 shard_map.130
  3.1 1.2 reshape.27
  4.3 30.6 %all-to-all-start = ((bf16[64,2,3200]{2,1,0:T(2,128)(2,1)}), bf16[64,2,3200]{2,1,0:T(2,128)(2,1)}, u32[]{:S(2)}, u32[]{:S(2)}) async-start(bf16[64,2,3200]{2,1,0:T(2,128)(2,1)} %reshape.27), calls=%async_computation | async-start | bytes 1638400 | tf_op jit(solution)/shard_map/all_to_all | solution.py:260
  34.9 2.4 collective-permute-start.1
  37.4 3.1 %collective-permute-start = (bf16[64,768]{1,0:T(8,128)(2,1)S(1)}, bf16[64,768]{1,0:T(8,128)(2,1)S(1)}, u32[]{:S(2)}, u32[]{:S(2)}) collective-permute-start(bf16[64,768]{1,0:T(8,128)(2,1)S(1)} %get-tuple-element.21), channel_id=1, source_target_pairs={{0,1},{1,2},{2,3},{3,4},{4,5},{5,6},{6,7},{7,8},{8,9},{9,10},{10,1... | collective-permute-start | bytes 294920 | tf_op jit(solution)/shard_map/ppermute | solution.py:265
  40.5 65.5 %collective-permute-done.1.high = bf16[64,768]{1,0:T(8,128)(2,1)S(1)} collective-permute-done((bf16[64,768]{1,0:T(8,128)(2,1)S(1)}, bf16[64,768]{1,0:T(8,128)(2,1)S(1)}, u32[]{:S(2)}, u32[]{:S(2)}) %collective-permute-start.1) | collective-permute-done | bytes 98336 | tf_op jit(solution)/shard_map/ppermute | solution.py:266
  106.0 1.4 shard_map.131
  107.5 0.8 copy-done.7
  108.3 15.7 %all-to-all-done = bf16[64,2,3200]{2,1,0:T(2,128)(2,1)} async-done(((bf16[64,2,3200]{2,1,0:T(2,128)(2,1)}), bf16[64,2,3200]{2,1,0:T(2,128)(2,1)}, u32[]{:S(2)}, u32[]{:S(2)}) %all-to-all-start) | async-done | bytes 819232 | tf_op jit(solution)/shard_map/all_to_all | solution.py:260
  124.0 2.4 reshape.28.arrived
  126.4 2.3 shard_map.132
  128.7 8.1 %all-to-all-start.1 = ((bf16[64,8,512]{2,1,0:T(8,128)(2,1)}), bf16[64,8,512]{2,1,0:T(8,128)(2,1)S(1)}, u32[]{:S(2)}, u32[]{:S(2)}) async-start(bf16[64,8,512]{2,1,0:T(8,128)(2,1)} %bitcast.6), calls=%async_computation.1 | async-start | bytes 1048576 | tf_op jit(solution)/shard_map/all_to_all | solution.py:283
  136.7 0.8 shard_map.133
  137.6 2.4 collective-permute-start.2
  140.0 1.3 collective-permute-done.2
  141.3 0.1 add_convert_fusion
  141.5 3.1 %collective-permute-start.3 = (bf16[96,512]{1,0:T(8,128)(2,1)S(1)}, bf16[96,512]{1,0:T(8,128)(2,1)S(1)}, u32[]{:S(2)}, u32[]{:S(2)}) collective-permute-start(bf16[96,512]{1,0:T(8,128)(2,1)S(1)} %get-tuple-element.17), channel_id=1, source_target_pairs={{0,256},{64,320},{128,384},{192,448},{256,512},{320,576},{384,640}... | collective-permute-start | bytes 294920 | tf_op jit(solution)/shard_map/ppermute | solution.py:173
  144.6 3.4 %collective-permute-start.5 = (bf16[96,512]{1,0:T(8,128)(2,1)S(1)}, bf16[96,512]{1,0:T(8,128)(2,1)S(1)}, u32[]{:S(2)}, u32[]{:S(2)}) collective-permute-start(bf16[96,512]{1,0:T(8,128)(2,1)S(1)} %get-tuple-element.18), channel_id=1, source_target_pairs={{0,768},{64,832},{128,896},{192,960},{256,0},{320,64},{384,128},{4... | collective-permute-start | bytes 294920 | tf_op jit(solution)/shard_map/ppermute | solution.py:173
  148.0 3.4 %collective-permute-start.4 = (bf16[96,512]{1,0:T(8,128)(2,1)S(1)}, bf16[96,512]{1,0:T(8,128)(2,1)S(1)}, u32[]{:S(2)}, u32[]{:S(2)}) collective-permute-start(bf16[96,512]{1,0:T(8,128)(2,1)S(1)} %get-tuple-element.19), channel_id=1, source_target_pairs={{0,512},{64,576},{128,640},{192,704},{256,768},{320,832},{384,896}... | collective-permute-start | bytes 294920 | tf_op jit(solution)/shard_map/ppermute | solution.py:173
  151.5 3.7 %collective-permute-done.4 = bf16[96,512]{1,0:T(8,128)(2,1)S(1)} collective-permute-done((bf16[96,512]{1,0:T(8,128)(2,1)S(1)}, bf16[96,512]{1,0:T(8,128)(2,1)S(1)}, u32[]{:S(2)}, u32[]{:S(2)}) %collective-permute-start.4) | collective-permute-done | bytes 98336 | tf_op jit(solution)/shard_map/ppermute | solution.py:173
  155.2 3.2 %collective-permute-start.6 = (bf16[24,512]{1,0:T(8,128)(2,1)S(1)}, bf16[24,512]{1,0:T(8,128)(2,1)S(1)}, u32[]{:S(2)}, u32[]{:S(2)}) collective-permute-start(bf16[24,512]{1,0:T(8,128)(2,1)S(1)} %get-tuple-element.22), channel_id=1, source_target_pairs={{0,64},{64,128},{128,192},{192,0},{256,320},{320,384},{384,448},{4... | collective-permute-start | bytes 73736 | tf_op jit(solution)/shard_map/ppermute | solution.py:173
  158.4 3.4 %collective-permute-start.8 = (bf16[24,512]{1,0:T(8,128)(2,1)S(1)}, bf16[24,512]{1,0:T(8,128)(2,1)S(1)}, u32[]{:S(2)}, u32[]{:S(2)}) collective-permute-start(bf16[24,512]{1,0:T(8,128)(2,1)S(1)} %get-tuple-element.23), channel_id=1, source_target_pairs={{0,192},{64,0},{128,64},{192,128},{256,448},{320,256},{384,320},{4... | collective-permute-start | bytes 73736 | tf_op jit(solution)/shard_map/ppermute | solution.py:173
  161.8 3.5 %collective-permute-start.7 = (bf16[24,512]{1,0:T(8,128)(2,1)S(1)}, bf16[24,512]{1,0:T(8,128)(2,1)S(1)}, u32[]{:S(2)}, u32[]{:S(2)}) collective-permute-start(bf16[24,512]{1,0:T(8,128)(2,1)S(1)} %get-tuple-element.24), channel_id=1, source_target_pairs={{0,128},{64,192},{128,0},{192,64},{256,384},{320,448},{384,256},{4... | collective-permute-start | bytes 73736 | tf_op jit(solution)/shard_map/ppermute | solution.py:173
  165.4 2.8 %collective-permute-done.7 = bf16[24,512]{1,0:T(8,128)(2,1)S(1)} collective-permute-done((bf16[24,512]{1,0:T(8,128)(2,1)S(1)}, bf16[24,512]{1,0:T(8,128)(2,1)S(1)}, u32[]{:S(2)}, u32[]{:S(2)}) %collective-permute-start.7) | collective-permute-done | bytes 24608 | tf_op jit(solution)/shard_map/ppermute | solution.py:173
  168.2 59.6 %all-gather = bf16[768,512]{1,0:T(8,128)(2,1)S(1)} all-gather(bf16[24,512]{1,0:T(8,128)(2,1)S(1)} %add_convert_fusion.2), channel_id=2, replica_groups={{0,2,4,6,8,10,12,14,16,18,20,22,24,26,28,30,32,34,36,38,40,42,44,46,48,..., dimensions={0}, use_global_device_ids=true | all-gather | bytes 811008 | tf_op jit(solution)/shard_map/all_gather | solution.py:204
  227.8 0.1 shard_map.134
  228.0 13.3 %all_to_all.15 = bf16[16,24,512]{2,1,0:T(8,128)(2,1)S(1)} all-to-all(bf16[16,24,512]{2,1,0:T(8,128)(2,1)S(1)} %shard_map.134), channel_id=1, replica_groups=mesh['grp'=16,'dev'=64] {'grp'}, dimensions={0} | all-to-all | bytes 786432 | tf_op jit(solution)/shard_map/all_to_all | solution.py:212
  241.2 16.0 %collective-permute-start.9 = (bf16[384,512]{1,0:T(8,128)(2,1)S(1)}, bf16[384,512]{1,0:T(8,128)(2,1)S(1)}, u32[]{:S(2)}, u32[]{:S(2)}) collective-permute-start(bf16[384,512]{1,0:T(8,128)(2,1)S(1)} %bitcast.12), channel_id=1, source_target_pairs={{0,1},{1,0},{2,3},{3,2},{4,5},{5,4},{6,7},{7,6},{8,9},{9,8},{10,11... | collective-permute-start | bytes 1179656 | tf_op jit(solution)/shard_map/ppermute | solution.py:182
  257.2 1.4 shard_map.135
  258.6 1.4 shard_map.136
  (31 shorter events, 0.2 us)
Async XLA Ops:
  1.4 1.0 copy-start.4
  3.1 31.8 %copy-start = (bf16[256,768]{1,0:T(8,128)(2,1)S(1)}, bf16[256,768]{1,0:T(8,128)(2,1)}, u32[]{:S(2)}) copy-start(bf16[256,768]{1,0:T(8,128)(2,1)} %papers.1) | copy-start | bytes 1179652
  3.1 102.9 %copy-start.1 = (bf16[768,512]{1,0:T(8,128)(2,1)S(1)}, bf16[768,512]{1,0:T(8,128)(2,1)}, u32[]{:S(2)}) copy-start(bf16[768,512]{1,0:T(8,128)(2,1)} %w_self.1) | copy-start | bytes 2359300
  3.1 102.9 %copy-start.2 = (bf16[768,512]{1,0:T(8,128)(2,1)S(1)}, bf16[768,512]{1,0:T(8,128)(2,1)}, u32[]{:S(2)}) copy-start(bf16[768,512]{1,0:T(8,128)(2,1)} %w_cite.1) | copy-start | bytes 2359300
  3.1 102.9 %copy-start.5 = (s32[256,8]{0,1:T(8,128)S(1)}, s32[256,8]{0,1:T(8,128)}, u32[]{:S(2)}) copy-start(s32[256,8]{0,1:T(8,128)} %param.18) | copy-start | bytes 24580
  3.1 102.9 %copy-start.6 = (f32[512]{0:T(512)S(1)}, f32[512]{0:T(512)}, u32[]{:S(2)}) copy-start(f32[512]{0:T(512)} %param.17) | copy-start | bytes 6148
  4.3 119.7 %all-to-all-start = ((bf16[64,2,3200]{2,1,0:T(2,128)(2,1)}), bf16[64,2,3200]{2,1,0:T(2,128)(2,1)}, u32[]{:S(2)}, u32[]{:S(2)}) async-start(bf16[64,2,3200]{2,1,0:T(2,128)(2,1)} %reshape.27), calls=%async_computation | async-start | bytes 1638400 | tf_op jit(solution)/shard_map/all_to_all | solution.py:260
  34.9 71.1 %collective-permute-start.1 = (bf16[64,768]{1,0:T(8,128)(2,1)S(1)}, bf16[64,768]{1,0:T(8,128)(2,1)S(1)}, u32[]{:S(2)}, u32[]{:S(2)}) collective-permute-start(bf16[64,768]{1,0:T(8,128)(2,1)S(1)} %get-tuple-element.20), channel_id=1, source_target_pairs={{1,0},{2,1},{3,2},{4,3},{5,4},{6,5},{7,6},{8,7},{9,8},{10,9},{11,1... | collective-permute-start | bytes 294920 | tf_op jit(solution)/shard_map/ppermute | solution.py:266
  37.4 68.6 %collective-permute-start = (bf16[64,768]{1,0:T(8,128)(2,1)S(1)}, bf16[64,768]{1,0:T(8,128)(2,1)S(1)}, u32[]{:S(2)}, u32[]{:S(2)}) collective-permute-start(bf16[64,768]{1,0:T(8,128)(2,1)S(1)} %get-tuple-element.21), channel_id=1, source_target_pairs={{0,1},{1,2},{2,3},{3,4},{4,5},{5,6},{6,7},{7,8},{8,9},{9,10},{10,1... | collective-permute-start | bytes 294920 | tf_op jit(solution)/shard_map/ppermute | solution.py:265
  107.5 0.8 copy-start.7
  108.3 18.1 %copy-start.3 = (bf16[768,512]{1,0:T(8,128)(2,1)S(1)}, bf16[768,512]{1,0:T(8,128)(2,1)}, u32[]{:S(2)}) copy-start(bf16[768,512]{1,0:T(8,128)(2,1)} %w_aut.3) | copy-start | bytes 2359300
  108.3 18.1 %copy-start.9 = (bf16[256,512]{1,0:T(8,128)(2,1)S(1)}, bf16[256,512]{1,0:T(8,128)(2,1)}, u32[]{:S(2)}) copy-start(bf16[256,512]{1,0:T(8,128)(2,1)} %cotangent.1) | copy-start | bytes 786436
  124.0 2.4 copy-start.8
  128.7 99.3 %all-to-all-start.1 = ((bf16[64,8,512]{2,1,0:T(8,128)(2,1)}), bf16[64,8,512]{2,1,0:T(8,128)(2,1)S(1)}, u32[]{:S(2)}, u32[]{:S(2)}) async-start(bf16[64,8,512]{2,1,0:T(8,128)(2,1)} %bitcast.6), calls=%async_computation.1 | async-start | bytes 1048576 | tf_op jit(solution)/shard_map/all_to_all | solution.py:283
  137.6 3.7 %collective-permute-start.2 = (bf16[384,512]{1,0:T(8,128)(2,1)S(1)}, bf16[384,512]{1,0:T(8,128)(2,1)S(1)}, u32[]{:S(2)}, u32[]{:S(2)}) collective-permute-start(bf16[384,512]{1,0:T(8,128)(2,1)S(1)} %constant_dynamic-slice_fusion.6), channel_id=1, source_target_pairs={{0,1},{1,0},{2,3},{3,2},{4,5},{5,4},{6,7},{7,6},{8,9},{9,8},{10,11... | collective-permute-start | bytes 1179656 | tf_op jit(solution)/shard_map/ppermute | solution.py:173
  141.5 10.0 %collective-permute-start.3 = (bf16[96,512]{1,0:T(8,128)(2,1)S(1)}, bf16[96,512]{1,0:T(8,128)(2,1)S(1)}, u32[]{:S(2)}, u32[]{:S(2)}) collective-permute-start(bf16[96,512]{1,0:T(8,128)(2,1)S(1)} %get-tuple-element.17), channel_id=1, source_target_pairs={{0,256},{64,320},{128,384},{192,448},{256,512},{320,576},{384,640}... | collective-permute-start | bytes 294920 | tf_op jit(solution)/shard_map/ppermute | solution.py:173
  144.6 6.9 %collective-permute-start.5 = (bf16[96,512]{1,0:T(8,128)(2,1)S(1)}, bf16[96,512]{1,0:T(8,128)(2,1)S(1)}, u32[]{:S(2)}, u32[]{:S(2)}) collective-permute-start(bf16[96,512]{1,0:T(8,128)(2,1)S(1)} %get-tuple-element.18), channel_id=1, source_target_pairs={{0,768},{64,832},{128,896},{192,960},{256,0},{320,64},{384,128},{4... | collective-permute-start | bytes 294920 | tf_op jit(solution)/shard_map/ppermute | solution.py:173
  148.0 7.2 %collective-permute-start.4 = (bf16[96,512]{1,0:T(8,128)(2,1)S(1)}, bf16[96,512]{1,0:T(8,128)(2,1)S(1)}, u32[]{:S(2)}, u32[]{:S(2)}) collective-permute-start(bf16[96,512]{1,0:T(8,128)(2,1)S(1)} %get-tuple-element.19), channel_id=1, source_target_pairs={{0,512},{64,576},{128,640},{192,704},{256,768},{320,832},{384,896}... | collective-permute-start | bytes 294920 | tf_op jit(solution)/shard_map/ppermute | solution.py:173
  155.2 10.1 %collective-permute-start.6 = (bf16[24,512]{1,0:T(8,128)(2,1)S(1)}, bf16[24,512]{1,0:T(8,128)(2,1)S(1)}, u32[]{:S(2)}, u32[]{:S(2)}) collective-permute-start(bf16[24,512]{1,0:T(8,128)(2,1)S(1)} %get-tuple-element.22), channel_id=1, source_target_pairs={{0,64},{64,128},{128,192},{192,0},{256,320},{320,384},{384,448},{4... | collective-permute-start | bytes 73736 | tf_op jit(solution)/shard_map/ppermute | solution.py:173
  158.4 6.9 %collective-permute-start.8 = (bf16[24,512]{1,0:T(8,128)(2,1)S(1)}, bf16[24,512]{1,0:T(8,128)(2,1)S(1)}, u32[]{:S(2)}, u32[]{:S(2)}) collective-permute-start(bf16[24,512]{1,0:T(8,128)(2,1)S(1)} %get-tuple-element.23), channel_id=1, source_target_pairs={{0,192},{64,0},{128,64},{192,128},{256,448},{320,256},{384,320},{4... | collective-permute-start | bytes 73736 | tf_op jit(solution)/shard_map/ppermute | solution.py:173
  161.8 6.4 %collective-permute-start.7 = (bf16[24,512]{1,0:T(8,128)(2,1)S(1)}, bf16[24,512]{1,0:T(8,128)(2,1)S(1)}, u32[]{:S(2)}, u32[]{:S(2)}) collective-permute-start(bf16[24,512]{1,0:T(8,128)(2,1)S(1)} %get-tuple-element.24), channel_id=1, source_target_pairs={{0,128},{64,192},{128,0},{192,64},{256,384},{320,448},{384,256},{4... | collective-permute-start | bytes 73736 | tf_op jit(solution)/shard_map/ppermute | solution.py:173
  241.2 17.4 %collective-permute-start.9 = (bf16[384,512]{1,0:T(8,128)(2,1)S(1)}, bf16[384,512]{1,0:T(8,128)(2,1)S(1)}, u32[]{:S(2)}, u32[]{:S(2)}) collective-permute-start(bf16[384,512]{1,0:T(8,128)(2,1)S(1)} %bitcast.12), channel_id=1, source_target_pairs={{0,1},{1,0},{2,3},{3,2},{4,5},{5,4},{6,7},{7,6},{8,9},{9,8},{10,11... | collective-permute-start | bytes 1179656 | tf_op jit(solution)/shard_map/ppermute | solution.py:182

commit v4 on v2

--- a/solution.py
+++ b/solution.py
@@ -54,7 +54,7 @@
 def pack_kernel(devs, cap, authors, ends, out):
     auts, width = authors.shape
     edges = ends.shape[1]
-    lines = out.shape[0]
+    lines = out.shape[0] * out.shape[1]
     side = cap // HALVES
     position = edge_slots(ends[0:1, :], devs, cap)
     author_edge = where_equal(iota((auts, edges), 0), ends[1:2, :])
@@ -66,9 +66,10 @@
         slot_edge = where_equal(line + q, position)
         picked.append(mm(slot_edge, author_edge, NT).astype(BF))
         aux = aux + mm(slot_edge, jnp.where(lane == q, rows, 0).astype(F32).astype(BF), NT)
-    out[:, side * width :] = aux.astype(BF)
+    out[:, :, side * width :] = aux.astype(BF).reshape(out.shape[0], HALVES, AUX)
     for q in range(side):
-        out[:, q * width : (q + 1) * width] = mm(picked[q], authors[...], NN).astype(BF)
+        rows_of = mm(picked[q], authors[...], NN).astype(BF)
+        out[:, :, q * width : (q + 1) * width] = rows_of.reshape(out.shape[0], HALVES, width)
 
 
 def base_kernel(devs, cap, papers, low, high, cite, w_self, w_cite, bias, ends, base, owner):
@@ -92,30 +93,25 @@
     owner[...] = mm(slot_edge, author_edge, NT).astype(BF)
 
 
-def split_match(arrived, width, rows):
-    lines = arrived.shape[0]
-    side = (arrived.shape[1] - AUX) // width
-    aux = arrived[:, side * width :].astype(F32)
+def split_match(aux, side, rows):
+    lines = aux.shape[0]
     wanted = iota((lines, rows), 1).astype(F32) + 1.0
     match = [where_equal(aux[:, q : q + 1], wanted) for q in range(side)]
-    return jnp.concatenate(match, axis=0), aux
-
-
-def side_rows(arrived, width):
-    side = (arrived.shape[1] - AUX) // width
-    return jnp.concatenate(
-        [arrived[:, q * width : (q + 1) * width] for q in range(side)], axis=0
-    )
-
-
-def node_kernel(arrived, base, cotangent, w_aut, updated, slot_grad, scaled_out):
+    return jnp.concatenate(match, axis=0)
+
+
+def node_kernel(arrived, base, cotangent, w_aut, updated, slot_grad, side_rows, side_grad):
     width = w_aut.shape[0]
     rows = base.shape[0]
     total = slot_grad.shape[0]
-    lines = arrived.shape[0]
+    lines = arrived.shape[0] * arrived.shape[1]
     side = total // lines
-    match, aux = split_match(arrived, width, rows)
-    messages = mm(side_rows(arrived, width), w_aut[...], NN).astype(BF)
+    aux = arrived[:, :, side * width :].reshape(lines, AUX).astype(F32)
+    match = split_match(aux, side, rows)
+    for q in range(side):
+        piece = arrived[:, :, q * width : (q + 1) * width].reshape(lines, width)
+        side_rows[q * lines : (q + 1) * lines, :] = piece
+    messages = mm(side_rows[...], w_aut[...], NN).astype(BF)
     aut_sum = mm(match, messages, TN)
     count = mm(match, jnp.ones((total, AUX), BF), TN)[:, :1]
     inverse = 1.0 / jnp.maximum(count, 1.0)
@@ -124,7 +120,7 @@
     updated[...] = (pre * sigma).astype(BF)
     delta = cotangent[...].astype(F32) * sigma * (1.0 + pre * (1.0 - sigma))
     scaled = (delta * inverse).astype(BF)
-    scaled_out[...] = scaled
+    side_grad[...] = mm(match, scaled, NN).astype(BF)
     spread = where_equal(iota((total, lines), 0) // side, iota((total, lines), 1))
     lanes = mm(spread, aux.astype(BF), NN)
     own_lane = iota((total, AUX), 1) == iota((total, AUX), 0) % side
@@ -133,16 +129,27 @@
     slot_grad[...] = mm(slot_match, scaled, NN).astype(BF)
 
 
-def weight_kernel(arrived, scaled, partial):
-    width = partial.shape[0]
-    match, _ = split_match(arrived, width, scaled.shape[0])
-    grads = mm(match, scaled[...], NN).astype(BF)
-    partial[...] = mm(side_rows(arrived, width), grads, TN).astype(BF)
+def weight_kernel(side_rows, side_grad, partial):
+    partial[...] = mm(side_rows[...], side_grad[...], TN).astype(BF)
 
 
 def author_kernel(returned, owner, w_aut, grad_authors):
     grad_proj = mm(owner[...], returned[...], TN).astype(BF)
     grad_authors[...] = mm(grad_proj, w_aut[...], NT).astype(BF)
+
+
+def sum_kernel(parts, copies):
+    total = parts[0].astype(F32)
+    for n in range(1, parts.shape[0]):
+        total = total + parts[n].astype(F32)
+    total = total.astype(BF)
+    for n in range(copies.shape[0]):
+        copies[n] = total
+
+
+def copy_kernel(parts, copies):
+    for n in range(copies.shape[0]):
+        copies[n] = parts[...]
 
 
 def spread_kernel(scale, side, blocks, out):
@@ -210,29 +217,28 @@
     while step < 2 * NEAR:
         part = half_sum(part, jnp.where(dev & step, 1, 0), "dev", along_dev(step))
         step = step * 2
-    far = [list(range(i, dev_count, step)) for i in range(step)]
-    part = jnp.sum(lax.all_gather(part, "dev", axis_index_groups=far, axis=0), axis=0)
     return part.astype(BF)
 
 
 def gather_weight(part, grp_count, dev_count, scale):
     near = 2 * NEAR
+    far = dev_count // near
     rows, lanes = part.shape
-    groups = [[b * near + i for i in range(near)] for b in range(dev_count // near)]
-    part = lax.all_to_all(
-        jnp.broadcast_to(part[None], (near, rows, lanes)),
-        "dev",
-        0,
-        0,
-        axis_index_groups=groups,
-        tiled=True,
-    )
-    blocks = lax.all_to_all(
-        jnp.broadcast_to(part[None], (grp_count, near, rows, lanes)), "grp", 0, 0, tiled=True
-    ).reshape(grp_count * near, rows, lanes)
+    shape = jax.ShapeDtypeStruct
+    apart = [list(range(i, dev_count, near)) for i in range(near)]
+    beside = [[b * near + i for i in range(near)] for b in range(far)]
+
+    def exchange(copies, axis, groups):
+        return lax.all_to_all(copies, axis, 0, 0, axis_index_groups=groups, tiled=True)
+
+    parts = exchange(jnp.broadcast_to(part[None], (far, rows, lanes)), "dev", apart)
+    (copies,) = call(sum_kernel, (shape((near, rows, lanes), BF),), (parts,), 0)
+    parts = exchange(copies, "dev", beside)
+    (copies,) = call(copy_kernel, (shape((grp_count, near, rows, lanes), BF),), (parts,), 0)
+    blocks = exchange(copies, "grp", None).reshape(grp_count * near, rows, lanes)
     side = math.isqrt(grp_count)
-    shape = jax.ShapeDtypeStruct((2 * grp_count * rows, NEAR * lanes), F32)
-    (whole,) = call(functools.partial(spread_kernel, scale, side), (shape,), (blocks,), 0)
+    whole_shape = shape((2 * grp_count * rows, NEAR * lanes), F32)
+    (whole,) = call(functools.partial(spread_kernel, scale, side), (whole_shape,), (blocks,), 0)
     return whole
 
 
@@ -264,13 +270,13 @@
 
     (outgoing,) = call(
         functools.partial(pack_kernel, dev_count, slots),
-        (shape((lines, line), BF),),
+        (shape((dev_count, HALVES, line), BF),),
         (authors, ends),
         2 * total * aut_rows * (edges + width),
     )
     arrived = lax.all_to_all(
-        outgoing.reshape(dev_count, HALVES, line), "dev", 0, 0, tiled=True
-    ).reshape(lines, line)
+        outgoing, "dev", 0, 0, tiled=True
+    )
     forward = [(i, i + 1) for i in range(dev_count - 1)]
     backward = [(i + 1, i) for i in range(dev_count - 1)]
     low = lax.ppermute(papers[pap_rows - RIM :], "dev", forward)
@@ -281,12 +287,13 @@
         (papers, low, high, cite_col.T, w_self, w_cite, bias.reshape(1, hidden), ends),
         2 * pap_rows * width * (2 * hidden + pap_rows + 2 * RIM),
     )
-    updated, slot_grad, scaled = call(
+    updated, slot_grad, side_rows, side_grad = call(
         node_kernel,
         (
             shape((pap_rows, hidden), BF),
             shape((total, hidden), BF),
-            shape((pap_rows, hidden), BF),
+            shape((total, width), BF),
+            shape((total, hidden), BF),
         ),
         (arrived, base, cotangent, w_aut),
         2 * total * hidden * (width + 2 * pap_rows),
@@ -297,7 +304,7 @@
     (partial,) = call(
         weight_kernel,
         (shape((width, hidden), BF),),
-        (arrived, scaled),
+        (side_rows, side_grad),
         2 * total * width * hidden,
     )
     part = reduce_weight(partial, grp_count, dev_count)

time: 266 us -> 265 us (level)
  waiting for transfers between devices: 110 us -> 127 us
  blocking collectives: 58.2 us -> 41.5 us
    ppermute x1, waiting for transfers between devices: 0.01 us -> 56.7 us  [per_device(): low = lax.ppermute(papers[pap_rows - RIM:], 'dev', forward)]
    ppermute x1, waiting for transfers between devices: 65.5 us -> 8.87 us  [per_device(): high = lax.ppermute(papers[:RIM], 'dev', backward)]
    all_gather x1 -> x0, blocking collectives: 42.7 us -> none  [reduce_weight(): lax.all_gather(part, 'dev', axis_index_groups=far, axis=0)]
    all_to_all x1 -> x2, blocking collectives: 15.5 us -> 41.5 us  [exchange(): lax.all_to_all(copies, axis, 0, 0, axis_index_groups=groups, tiled=True)]
    all_to_all x1, waiting for transfers between devices: 0.01 us -> 15.8 us  [per_device(): lax.all_to_all(slot_grad.reshape(dev_count, slots, hidden), 'dev', 0, 0,...]
    reshape x2 -> x0, local copies, waits for them, and re-layouts: 3.58 us -> none  [the longest x1 2.38 us: per_device(): arrived = lax.all_to_all(outgoing.reshape(dev_count, HALVES, line), 'dev'...]
    pallas_call x6 -> x8, Pallas kernels: 7.88 us -> 9.89 us  [call(): pl.pallas_call(kernel, out_shape=outs, compiler_params=pltpu.CompilerPara...]
  transfers between devices with their start and end apart: 14 -> 14, of which waited for: 8 -> 12; matrix products, arithmetic and copies ran while one was open for 0% -> 0% of each run, Pallas kernels for 1% -> 1%
where the time goes in v4:
time: 265 us; the launch traced here: 264 us
  waiting for transfers between devices  127 us (48%)
  starting transfers between devices  79.3 us (30%)
  blocking collectives  41.5 us (16%)
  Pallas kernels  9.89 us (4%)
  local copies, waits for them, and re-layouts  4.13 us (2%)
    ppermute x1, waiting for transfers between devices, per_device(): low = lax.ppermute(papers[pap_rows - RIM:], 'dev', forward)  56.7 us
    all_to_all x2, blocking collectives, exchange(): lax.all_to_all(copies, axis, 0, 0, axis_index_groups=groups, tiled=True)  41.5 us
    all_to_all x1, starting transfers between devices, per_device(): arrived = lax.all_to_all(outgoing, 'dev', 0, 0, tiled=True)  30.4 us
    ppermute x7, starting transfers between devices, shift_sum(): lax.ppermute(piece(lax.rem(place + k, count)), axis, perm(k))  21.3 us
    all_to_all x1, waiting for transfers between devices, per_device(): lax.all_to_all(slot_grad.reshape(dev_count, slots, hidden), 'dev', 0, 0,...  15.8 us
    all_to_all x1, waiting for transfers between devices, per_device(): arrived = lax.all_to_all(outgoing, 'dev', 0, 0, tiled=True)  15.7 us
    all_to_all x1, waiting for transfers between devices, exchange(): lax.all_to_all(copies, axis, 0, 0, axis_index_groups=groups, tiled=True)  11.3 us
    pallas_call x8, Pallas kernels, call(): pl.pallas_call(kernel, out_shape=outs, compiler_params=pltpu.CompilerPara...  9.89 us
  transfers between devices with their start and end apart: 14, of which 12 were waited for; matrix products, arithmetic and copies ran while one was open for 0% of the time, Pallas kernels for 1%

profile of v4, /device:TPU:1, one launch (start us, length us, event | category | flops | bytes accessed | tf_op | source)
XLA Modules:
  0.0 264.0 jit_solution(11138002914939071748)
XLA Ops:
  2.4 1.6 shard_map.130
  4.0 30.4 %all-to-all-start = ((bf16[64,2,3200]{2,1,0:T(2,128)(2,1)}), bf16[64,2,3200]{2,1,0:T(2,128)(2,1)S(1)}, u32[]{:S(2)}, u32[]{:S(2)}) async-start(bf16[64,2,3200]{2,1,0:T(2,128)(2,1)} %shard_map.130), calls=%async_computation | async-start | bytes 1638400 | tf_op jit(solution)/shard_map/all_to_all | solution.py:277
  34.5 3.7 %collective-permute-start = (bf16[64,768]{1,0:T(8,128)(2,1)S(1)}, bf16[64,768]{1,0:T(8,128)(2,1)S(1)}, u32[]{:S(2)}, u32[]{:S(2)}) collective-permute-start(bf16[64,768]{1,0:T(8,128)(2,1)S(1)} %get-tuple-element.23), channel_id=1, source_target_pairs={{0,1},{1,2},{2,3},{3,4},{4,5},{5,6},{6,7},{7,8},{8,9},{9,10},{10,1... | collective-permute-start | bytes 294920 | tf_op jit(solution)/shard_map/ppermute | solution.py:282
  38.2 1.9 collective-permute-start.1
  40.1 56.7 %collective-permute-done.low = bf16[64,768]{1,0:T(8,128)(2,1)S(1)} collective-permute-done((bf16[64,768]{1,0:T(8,128)(2,1)S(1)}, bf16[64,768]{1,0:T(8,128)(2,1)S(1)}, u32[]{:S(2)}, u32[]{:S(2)}) %collective-permute-start) | collective-permute-done | bytes 98336 | tf_op jit(solution)/shard_map/ppermute | solution.py:282
  96.7 8.9 %collective-permute-done.1.high = bf16[64,768]{1,0:T(8,128)(2,1)S(1)} collective-permute-done((bf16[64,768]{1,0:T(8,128)(2,1)S(1)}, bf16[64,768]{1,0:T(8,128)(2,1)S(1)}, u32[]{:S(2)}, u32[]{:S(2)}) %collective-permute-start.1) | collective-permute-done | bytes 98336 | tf_op jit(solution)/shard_map/ppermute | solution.py:283
  105.6 1.4 shard_map.131
  107.9 15.7 %all-to-all-done.arrived = bf16[64,2,3200]{2,1,0:T(2,128)(2,1)S(1)} async-done(((bf16[64,2,3200]{2,1,0:T(2,128)(2,1)}), bf16[64,2,3200]{2,1,0:T(2,128)(2,1)S(1)}, u32[]{:S(2)}, u32[]{:S(2)}) %all-to-all-start) | async-done | bytes 819232 | tf_op jit(solution)/shard_map/all_to_all | solution.py:277
  125.8 2.6 shard_map.132
  128.4 8.1 %all-to-all-start.1 = ((bf16[64,8,512]{2,1,0:T(8,128)(2,1)}), bf16[64,8,512]{2,1,0:T(8,128)(2,1)S(1)}, u32[]{:S(2)}, u32[]{:S(2)}) async-start(bf16[64,8,512]{2,1,0:T(8,128)(2,1)} %bitcast.5), calls=%async_computation.1 | async-start | bytes 1048576 | tf_op jit(solution)/shard_map/all_to_all | solution.py:301
  137.1 2.4 collective-permute-start.2
  139.5 1.3 collective-permute-done.2
  140.9 4.4 %collective-permute-start.5 = (bf16[96,512]{1,0:T(8,128)(2,1)S(1)}, bf16[96,512]{1,0:T(8,128)(2,1)S(1)}, u32[]{:S(2)}, u32[]{:S(2)}) collective-permute-start(bf16[96,512]{1,0:T(8,128)(2,1)S(1)} %get-tuple-element.20), channel_id=1, source_target_pairs={{0,768},{64,832},{128,896},{192,960},{256,0},{320,64},{384,128},{4... | collective-permute-start | bytes 294920 | tf_op jit(solution)/shard_map/ppermute | solution.py:178
  145.4 2.4 collective-permute-start.4
  147.8 2.5 collective-permute-start.3
  150.3 2.2 collective-permute-done.4
  152.5 2.3 collective-permute-done.3
  154.9 4.8 %collective-permute-start.8 = (bf16[24,512]{1,0:T(8,128)(2,1)S(1)}, bf16[24,512]{1,0:T(8,128)(2,1)S(1)}, u32[]{:S(2)}, u32[]{:S(2)}) collective-permute-start(bf16[24,512]{1,0:T(8,128)(2,1)S(1)} %get-tuple-element.25), channel_id=1, source_target_pairs={{0,192},{64,0},{128,64},{192,128},{256,448},{320,256},{384,320},{4... | collective-permute-start | bytes 73736 | tf_op jit(solution)/shard_map/ppermute | solution.py:178
  159.7 2.3 collective-permute-start.7
  161.9 2.6 collective-permute-start.6
  164.6 1.5 collective-permute-done.7
  166.0 2.0 collective-permute-done.6
  168.1 3.2 %collective-permute-start.9 = (f32[24,256]{1,0:T(8,128)S(1)}, f32[24,256]{1,0:T(8,128)S(1)}, u32[]{:S(2)}, u32[]{:S(2)}) collective-permute-start(f32[24,256]{1,0:T(8,128)S(1)} %constant_dynamic-slice_fusion.1), channel_id=1, source_target_pairs={{0,2},{1,3},{2,0},{3,1},{4,6},{5,7},{6,4},{7,5},{8,10},{9,11},{10,... | collective-permute-start | bytes 73736 | tf_op jit(solution)/shard_map/ppermute | solution.py:194
  171.3 7.9 %collective-permute-done.9 = f32[24,256]{1,0:T(8,128)S(1)} collective-permute-done((f32[24,256]{1,0:T(8,128)S(1)}, f32[24,256]{1,0:T(8,128)S(1)}, u32[]{:S(2)}, u32[]{:S(2)}) %collective-permute-start.9) | collective-permute-done | bytes 24608 | tf_op jit(solution)/shard_map/ppermute | solution.py:194
  179.2 3.9 %collective-permute-start.10 = (f32[24,128]{1,0:T(8,128)S(1)}, f32[24,128]{1,0:T(8,128)S(1)}, u32[]{:S(2)}, u32[]{:S(2)}) collective-permute-start(f32[24,128]{1,0:T(8,128)S(1)} %constant_dynamic-slice_fusion), channel_id=1, source_target_pairs={{0,4},{1,5},{2,6},{3,7},{4,0},{5,1},{6,2},{7,3},{8,12},{9,13},{10,... | collective-permute-start | bytes 36872 | tf_op jit(solution)/shard_map/ppermute | solution.py:194
  183.1 1.8 collective-permute-done.10
  184.9 15.8 %all-to-all-done.1 = bf16[64,8,512]{2,1,0:T(8,128)(2,1)S(1)} async-done(((bf16[64,8,512]{2,1,0:T(8,128)(2,1)}), bf16[64,8,512]{2,1,0:T(8,128)(2,1)S(1)}, u32[]{:S(2)}, u32[]{:S(2)}) %all-to-all-start.1) | async-done | bytes 524320 | tf_op jit(solution)/shard_map/all_to_all | solution.py:301
  200.8 31.5 %all_to_all.25.parts = bf16[8,24,128]{2,1,0:T(8,128)(2,1)S(1)} all-to-all(bf16[8,24,128]{2,1,0:T(8,128)(2,1)S(1)} %broadcast_in_dim.2), channel_id=1, replica_groups={{0,8,16,24,32,40,48,56},{1,9,17,25,33,41,49,57},{2,10,18,26,34,42,50,58..., dimensions={0} | all-to-all | bytes 98304 | tf_op jit(solution)/shard_map/all_to_all | solution.py:232
  232.3 10.0 %all_to_all.26.parts = bf16[8,24,128]{2,1,0:T(8,128)(2,1)S(1)} all-to-all(bf16[8,24,128]{2,1,0:T(8,128)(2,1)S(1)} %shard_map.135), channel_id=1, replica_groups={{0,1,2,3,4,5,6,7},{8,9,10,11,12,13,14,15},{16,17,18,19,20,21,22,23},{24..., dimensions={0} | all-to-all | bytes 98304 | tf_op jit(solution)/shard_map/all_to_all | solution.py:232
  243.3 6.8 %all-to-all-start.4 = ((bf16[16,8,24,128]{3,2,1,0:T(8,128)(2,1)}), bf16[16,8,24,128]{3,2,1,0:T(8,128)(2,1)S(1)}, u32[]{:S(2)}, u32[]{:S(2)}) async-start(bf16[16,8,24,128]{3,2,1,0:T(8,128)(2,1)} %shard_map.136), calls=%async_computation.4 | async-start | bytes 1572864 | tf_op jit(solution)/shard_map/all_to_all | solution.py:232
  250.0 1.4 shard_map.134
  251.4 11.3 %all-to-all-done.4 = bf16[16,8,24,128]{3,2,1,0:T(8,128)(2,1)S(1)} async-done(((bf16[16,8,24,128]{3,2,1,0:T(8,128)(2,1)}), bf16[16,8,24,128]{3,2,1,0:T(8,128)(2,1)S(1)}, u32[]{:S(2)}, u32[]{:S(2)}) %all-to-all-start.4) | async-done | bytes 786464 | tf_op jit(solution)/shard_map/all_to_all | solution.py:232
  (41 shorter events, 7.9 us)
Async XLA Ops:
  0.6 33.8 %copy-start = (bf16[256,768]{1,0:T(8,128)(2,1)S(1)}, bf16[256,768]{1,0:T(8,128)(2,1)}, u32[]{:S(2)}) copy-start(bf16[256,768]{1,0:T(8,128)(2,1)} %papers.1) | copy-start | bytes 1179652
  1.4 1.0 copy-start.5
  2.4 103.2 %copy-start.1 = (bf16[768,512]{1,0:T(8,128)(2,1)S(1)}, bf16[768,512]{1,0:T(8,128)(2,1)}, u32[]{:S(2)}) copy-start(bf16[768,512]{1,0:T(8,128)(2,1)} %w_self.1) | copy-start | bytes 2359300
  2.4 103.2 %copy-start.2 = (bf16[768,512]{1,0:T(8,128)(2,1)S(1)}, bf16[768,512]{1,0:T(8,128)(2,1)}, u32[]{:S(2)}) copy-start(bf16[768,512]{1,0:T(8,128)(2,1)} %w_cite.1) | copy-start | bytes 2359300
  2.4 103.2 %copy-start.6 = (s32[256,8]{0,1:T(8,128)S(1)}, s32[256,8]{0,1:T(8,128)}, u32[]{:S(2)}) copy-start(s32[256,8]{0,1:T(8,128)} %param.18) | copy-start | bytes 24580
  2.4 103.2 %copy-start.7 = (f32[512]{0:T(512)S(1)}, f32[512]{0:T(512)}, u32[]{:S(2)}) copy-start(f32[512]{0:T(512)} %param.17) | copy-start | bytes 6148
  4.0 119.6 %all-to-all-start = ((bf16[64,2,3200]{2,1,0:T(2,128)(2,1)}), bf16[64,2,3200]{2,1,0:T(2,128)(2,1)S(1)}, u32[]{:S(2)}, u32[]{:S(2)}) async-start(bf16[64,2,3200]{2,1,0:T(2,128)(2,1)} %shard_map.130), calls=%async_computation | async-start | bytes 1638400 | tf_op jit(solution)/shard_map/all_to_all | solution.py:277
  34.4 89.1 %copy-start.10 = (bf16[256,512]{1,0:T(8,128)(2,1)S(1)}, bf16[256,512]{1,0:T(8,128)(2,1)}, u32[]{:S(2)}) copy-start(bf16[256,512]{1,0:T(8,128)(2,1)} %cotangent.1) | copy-start | bytes 786436
  34.5 62.3 %collective-permute-start = (bf16[64,768]{1,0:T(8,128)(2,1)S(1)}, bf16[64,768]{1,0:T(8,128)(2,1)S(1)}, u32[]{:S(2)}, u32[]{:S(2)}) collective-permute-start(bf16[64,768]{1,0:T(8,128)(2,1)S(1)} %get-tuple-element.23), channel_id=1, source_target_pairs={{0,1},{1,2},{2,3},{3,4},{4,5},{5,6},{6,7},{7,8},{8,9},{9,10},{10,1... | collective-permute-start | bytes 294920 | tf_op jit(solution)/shard_map/ppermute | solution.py:282
  38.2 67.5 %collective-permute-start.1 = (bf16[64,768]{1,0:T(8,128)(2,1)S(1)}, bf16[64,768]{1,0:T(8,128)(2,1)S(1)}, u32[]{:S(2)}, u32[]{:S(2)}) collective-permute-start(bf16[64,768]{1,0:T(8,128)(2,1)S(1)} %get-tuple-element.22), channel_id=1, source_target_pairs={{1,0},{2,1},{3,2},{4,3},{5,4},{6,5},{7,6},{8,7},{9,8},{10,9},{11,1... | collective-permute-start | bytes 294920 | tf_op jit(solution)/shard_map/ppermute | solution.py:283
  107.1 0.8 copy-start.8
  123.6 1.1 copy-start.3
  124.7 1.0 copy-start.9
  128.4 72.4 %all-to-all-start.1 = ((bf16[64,8,512]{2,1,0:T(8,128)(2,1)}), bf16[64,8,512]{2,1,0:T(8,128)(2,1)S(1)}, u32[]{:S(2)}, u32[]{:S(2)}) async-start(bf16[64,8,512]{2,1,0:T(8,128)(2,1)} %bitcast.5), calls=%async_computation.1 | async-start | bytes 1048576 | tf_op jit(solution)/shard_map/all_to_all | solution.py:301
  137.1 3.7 %collective-permute-start.2 = (bf16[384,512]{1,0:T(8,128)(2,1)S(1)}, bf16[384,512]{1,0:T(8,128)(2,1)S(1)}, u32[]{:S(2)}, u32[]{:S(2)}) collective-permute-start(bf16[384,512]{1,0:T(8,128)(2,1)S(1)} %constant_dynamic-slice_fusion.8), channel_id=1, source_target_pairs={{0,1},{1,0},{2,3},{3,2},{4,5},{5,4},{6,7},{7,6},{8,9},{9,8},{10,11... | collective-permute-start | bytes 1179656 | tf_op jit(solution)/shard_map/ppermute | solution.py:178
  140.9 9.4 %collective-permute-start.5 = (bf16[96,512]{1,0:T(8,128)(2,1)S(1)}, bf16[96,512]{1,0:T(8,128)(2,1)S(1)}, u32[]{:S(2)}, u32[]{:S(2)}) collective-permute-start(bf16[96,512]{1,0:T(8,128)(2,1)S(1)} %get-tuple-element.20), channel_id=1, source_target_pairs={{0,768},{64,832},{128,896},{192,960},{256,0},{320,64},{384,128},{4... | collective-permute-start | bytes 294920 | tf_op jit(solution)/shard_map/ppermute | solution.py:178
  145.4 7.2 %collective-permute-start.4 = (bf16[96,512]{1,0:T(8,128)(2,1)S(1)}, bf16[96,512]{1,0:T(8,128)(2,1)S(1)}, u32[]{:S(2)}, u32[]{:S(2)}) collective-permute-start(bf16[96,512]{1,0:T(8,128)(2,1)S(1)} %get-tuple-element.21), channel_id=1, source_target_pairs={{0,512},{64,576},{128,640},{192,704},{256,768},{320,832},{384,896}... | collective-permute-start | bytes 294920 | tf_op jit(solution)/shard_map/ppermute | solution.py:178
  147.8 7.0 %collective-permute-start.3 = (bf16[96,512]{1,0:T(8,128)(2,1)S(1)}, bf16[96,512]{1,0:T(8,128)(2,1)S(1)}, u32[]{:S(2)}, u32[]{:S(2)}) collective-permute-start(bf16[96,512]{1,0:T(8,128)(2,1)S(1)} %get-tuple-element.19), channel_id=1, source_target_pairs={{0,256},{64,320},{128,384},{192,448},{256,512},{320,576},{384,640}... | collective-permute-start | bytes 294920 | tf_op jit(solution)/shard_map/ppermute | solution.py:178
  154.9 95.1 %copy-start.4 = (bf16[768,512]{1,0:T(8,128)(2,1)S(1)}, bf16[768,512]{1,0:T(8,128)(2,1)}, u32[]{:S(2)}) copy-start(bf16[768,512]{1,0:T(8,128)(2,1)} %w_aut.3) | copy-start | bytes 2359300
  154.9 9.7 %collective-permute-start.8 = (bf16[24,512]{1,0:T(8,128)(2,1)S(1)}, bf16[24,512]{1,0:T(8,128)(2,1)S(1)}, u32[]{:S(2)}, u32[]{:S(2)}) collective-permute-start(bf16[24,512]{1,0:T(8,128)(2,1)S(1)} %get-tuple-element.25), channel_id=1, source_target_pairs={{0,192},{64,0},{128,64},{192,128},{256,448},{320,256},{384,320},{4... | collective-permute-start | bytes 73736 | tf_op jit(solution)/shard_map/ppermute | solution.py:178
  159.7 6.4 %collective-permute-start.7 = (bf16[24,512]{1,0:T(8,128)(2,1)S(1)}, bf16[24,512]{1,0:T(8,128)(2,1)S(1)}, u32[]{:S(2)}, u32[]{:S(2)}) collective-permute-start(bf16[24,512]{1,0:T(8,128)(2,1)S(1)} %get-tuple-element.26), channel_id=1, source_target_pairs={{0,128},{64,192},{128,0},{192,64},{256,384},{320,448},{384,256},{4... | collective-permute-start | bytes 73736 | tf_op jit(solution)/shard_map/ppermute | solution.py:178
  161.9 6.1 %collective-permute-start.6 = (bf16[24,512]{1,0:T(8,128)(2,1)S(1)}, bf16[24,512]{1,0:T(8,128)(2,1)S(1)}, u32[]{:S(2)}, u32[]{:S(2)}) collective-permute-start(bf16[24,512]{1,0:T(8,128)(2,1)S(1)} %get-tuple-element.24), channel_id=1, source_target_pairs={{0,64},{64,128},{128,192},{192,0},{256,320},{320,384},{384,448},{4... | collective-permute-start | bytes 73736 | tf_op jit(solution)/shard_map/ppermute | solution.py:178
  168.1 11.1 %collective-permute-start.9 = (f32[24,256]{1,0:T(8,128)S(1)}, f32[24,256]{1,0:T(8,128)S(1)}, u32[]{:S(2)}, u32[]{:S(2)}) collective-permute-start(f32[24,256]{1,0:T(8,128)S(1)} %constant_dynamic-slice_fusion.1), channel_id=1, source_target_pairs={{0,2},{1,3},{2,0},{3,1},{4,6},{5,7},{6,4},{7,5},{8,10},{9,11},{10,... | collective-permute-start | bytes 73736 | tf_op jit(solution)/shard_map/ppermute | solution.py:194
  179.2 5.7 %collective-permute-start.10 = (f32[24,128]{1,0:T(8,128)S(1)}, f32[24,128]{1,0:T(8,128)S(1)}, u32[]{:S(2)}, u32[]{:S(2)}) collective-permute-start(f32[24,128]{1,0:T(8,128)S(1)} %constant_dynamic-slice_fusion), channel_id=1, source_target_pairs={{0,4},{1,5},{2,6},{3,7},{4,0},{5,1},{6,2},{7,3},{8,12},{9,13},{10,... | collective-permute-start | bytes 36872 | tf_op jit(solution)/shard_map/ppermute | solution.py:194
  243.3 19.5 %all-to-all-start.4 = ((bf16[16,8,24,128]{3,2,1,0:T(8,128)(2,1)}), bf16[16,8,24,128]{3,2,1,0:T(8,128)(2,1)S(1)}, u32[]{:S(2)}, u32[]{:S(2)}) async-start(bf16[16,8,24,128]{3,2,1,0:T(8,128)(2,1)} %shard_map.136), calls=%async_computation.4 | async-start | bytes 1572864 | tf_op jit(solution)/shard_map/all_to_all | solution.py:232

commit v5 on v4

--- a/solution.py
+++ b/solution.py
@@ -12,7 +12,6 @@
 K_CIT = 8
 AUX = 128
 HALVES = 2
-NEAR = 4
 BF = jnp.bfloat16
 F32 = jnp.float32
 NN = (((1,), (0,)), ((), ()))
@@ -138,32 +137,30 @@
     grad_authors[...] = mm(grad_proj, w_aut[...], NT).astype(BF)
 
 
-def sum_kernel(parts, copies):
-    total = parts[0].astype(F32)
-    for n in range(1, parts.shape[0]):
-        total = total + parts[n].astype(F32)
-    total = total.astype(BF)
-    for n in range(copies.shape[0]):
-        copies[n] = total
-
-
-def copy_kernel(parts, copies):
-    for n in range(copies.shape[0]):
-        copies[n] = parts[...]
-
-
-def spread_kernel(scale, side, blocks, out):
-    count, rows, lanes = blocks.shape
-    near = count // (side * side)
-    halves = near // 2
-    for n in range(count):
-        group, place = n // near, n % near
-        core, z = place % 2, place // 2
-        at = (core * side * side + group) * rows
-        column = 0
-        for bit in range(halves.bit_length() - 1):
-            column = column * 2 + (z >> bit & 1)
-        out[at : at + rows, column * lanes : (column + 1) * lanes] = blocks[n].astype(F32) * scale
+def ring_kernel(every, out):
+    total = every[0].astype(F32)
+    for n in range(1, every.shape[0]):
+        total = total + every[n].astype(F32)
+    out[...] = total.astype(BF)
+
+
+def join_kernel(own, other, bit, out):
+    half = own.shape[1]
+    first = bit[0] == 0
+    mine, came = own[...].astype(F32), other[...].astype(F32)
+    left = jnp.where(first, mine, came).astype(BF)
+    right = jnp.where(first, came, mine).astype(BF)
+    for n in range(out.shape[0]):
+        out[n, :, :half] = left
+        out[n, :, half:] = right
+
+
+def spread_kernel(scale, own, other, core, out):
+    half = own.shape[0]
+    first = core[0] == 0
+    mine, came = own[...].astype(F32) * scale, other[...].astype(F32) * scale
+    out[:half, :] = jnp.where(first, mine, came)
+    out[half:, :] = jnp.where(first, came, mine)
 
 
 def shift_sum(block, place, count, axis, perm):
@@ -183,7 +180,7 @@
     return total
 
 
-def half_sum(block, bit, axis, perm):
+def half_sum(block, bit, perm):
     size = block.shape[1] // 2
 
     def piece(at):
@@ -191,14 +188,28 @@
             block, (0, at * size), (block.shape[0], size), allow_negative_indices=False
         )
 
-    came = lax.ppermute(piece(1 - bit), axis, perm)
-    return piece(bit).astype(F32) + came.astype(F32)
+    came = lax.ppermute(piece(1 - bit), "dev", perm)
+    return piece(bit) + came
+
+
+def swap(block, step):
+    return lax.ppermute(block, "dev", [(d, d ^ step) for d in range(lax.axis_size("dev"))])
+
+
+def with_bit(kernel, out, own, other, bit):
+    vmem = pl.BlockSpec(memory_space=pltpu.VMEM)
+    return pl.pallas_call(
+        kernel,
+        out_shape=out,
+        in_specs=[vmem, vmem, pl.BlockSpec(memory_space=pltpu.SMEM)],
+        compiler_params=pltpu.CompilerParams(vmem_limit_bytes=16 * 1024 * 1024),
+    )(own, other, bit.reshape(1))
 
 
 def reduce_weight(partial, grp_count, dev_count):
     side = math.isqrt(grp_count)
     grp = lax.axis_index("grp")
-    dev = lax.axis_index("dev")
+    core = lax.axis_index("dev") & 1
     x, y = lax.div(grp, side), lax.rem(grp, side)
 
     def along_x(k):
@@ -207,39 +218,30 @@
     def along_y(k):
         return [(g, g // side * side + (g % side + k) % side) for g in range(grp_count)]
 
-    def along_dev(k):
+    def along_core(k):
         return [(d, d ^ k) for d in range(dev_count)]
 
-    part = shift_sum(partial, dev & 1, 2, "dev", lambda k: along_dev(k)).astype(BF)
+    part = shift_sum(partial, core, 2, "dev", along_core).astype(BF)
     part = shift_sum(part, x, side, "grp", along_x).astype(BF)
     part = shift_sum(part, y, side, "grp", along_y)
-    step = 2
-    while step < 2 * NEAR:
-        part = half_sum(part, jnp.where(dev & step, 1, 0), "dev", along_dev(step))
-        step = step * 2
-    return part.astype(BF)
-
-
-def gather_weight(part, grp_count, dev_count, scale):
-    near = 2 * NEAR
-    far = dev_count // near
-    rows, lanes = part.shape
+    bit = (lax.axis_index("dev") >> 1) & 1
+    part = half_sum(part, bit, along_core(2)).astype(BF)
+    ring = [list(range(i, dev_count, 4)) for i in range(4)]
+    every = lax.all_gather(part, "dev", axis_index_groups=ring, axis=0)
     shape = jax.ShapeDtypeStruct
-    apart = [list(range(i, dev_count, near)) for i in range(near)]
-    beside = [[b * near + i for i in range(near)] for b in range(far)]
-
-    def exchange(copies, axis, groups):
-        return lax.all_to_all(copies, axis, 0, 0, axis_index_groups=groups, tiled=True)
-
-    parts = exchange(jnp.broadcast_to(part[None], (far, rows, lanes)), "dev", apart)
-    (copies,) = call(sum_kernel, (shape((near, rows, lanes), BF),), (parts,), 0)
-    parts = exchange(copies, "dev", beside)
-    (copies,) = call(copy_kernel, (shape((grp_count, near, rows, lanes), BF),), (parts,), 0)
-    blocks = exchange(copies, "grp", None).reshape(grp_count * near, rows, lanes)
-    side = math.isqrt(grp_count)
-    whole_shape = shape((2 * grp_count * rows, NEAR * lanes), F32)
-    (whole,) = call(functools.partial(spread_kernel, scale, side), (whole_shape,), (blocks,), 0)
-    return whole
+    (own,) = call(ring_kernel, (shape(part.shape, BF),), (every,), 0)
+    rows, half = part.shape
+    return with_bit(
+        join_kernel, shape((grp_count, rows, 2 * half), BF), own, swap(own, 2), bit
+    )
+
+
+def gather_weight(own, scale):
+    grp_count, rows, lanes = own.shape
+    own = own.reshape(grp_count * rows, lanes)
+    out = jax.ShapeDtypeStruct((2 * grp_count * rows, lanes), F32)
+    core = lax.axis_index("dev") & 1
+    return with_bit(functools.partial(spread_kernel, scale), out, own, swap(own, 1), core)
 
 
 def per_device(
@@ -307,16 +309,18 @@
         (side_rows, side_grad),
         2 * total * width * hidden,
     )
-    part = reduce_weight(partial, grp_count, dev_count)
-    part, returned = lax.optimization_barrier((part, returned))
+    copies = reduce_weight(partial, grp_count, dev_count)
+    copies, returned = lax.optimization_barrier((copies, returned))
+    own = lax.all_to_all(copies, "grp", 0, 0, tiled=True)
     (grad_authors,) = call(
         author_kernel,
         (shape((aut_rows, width), BF),),
         (returned, owner, w_aut),
         2 * aut_rows * hidden * (total + width),
     )
+    own, grad_authors = lax.optimization_barrier((own, grad_authors))
     scale = 1.0 / math.sqrt(grp_count * dev_count * aut_rows)
-    grad_w_aut = gather_weight(part, grp_count, dev_count, scale)
+    grad_w_aut = gather_weight(own, scale)
     return (updated, grad_authors, grad_w_aut)
 
 

time: 265 us -> 252 us (0.951)
  waiting for transfers between devices: 127 us -> 109 us
  starting transfers between devices: 79.3 us -> 89.6 us
  blocking collectives: 41.5 us -> 36.7 us
    all_to_all x2 -> x0, blocking collectives: 41.5 us -> none  [exchange(): lax.all_to_all(copies, axis, 0, 0, axis_index_groups=groups, tiled=True)]
    all_gather x0 -> x1, blocking collectives: none -> 36.7 us  [reduce_weight(): every = lax.all_gather(part, 'dev', axis_index_groups=ring, axis=0)]
    all_to_all x1, waiting for transfers between devices: 15.8 us -> 0.01 us  [per_device(): lax.all_to_all(slot_grad.reshape(dev_count, slots, hidden), 'dev', 0, 0,...]
    ppermute x2 -> x3, starting transfers between devices: 7.15 us -> 17.5 us  [the longest x2 14.3 us: swap(): lax.ppermute(block, 'dev', [(d, d ^ step) for d in range(lax.axis_size('d...]
    all_to_all x1, waiting for transfers between devices: 11.3 us -> 6.58 us  [per_device(): own = lax.all_to_all(copies, 'grp', 0, 0, tiled=True)]
    pallas_call x8 -> x6, Pallas kernels: 9.89 us -> 7.67 us  [call(): pl.pallas_call(kernel, out_shape=outs, compiler_params=pltpu.CompilerPara...]
    ppermute x2 -> x3, waiting for transfers between devices: 9.66 us -> 11.6 us  [the longest x1 7.91 us: half_sum(): came = lax.ppermute(piece(1 - bit), 'dev', perm)]
  transfers between devices with their start and end apart: 14 -> 15, of which waited for: 12 -> 12; matrix products, arithmetic and copies ran while one was open for 0% -> 0% of each run, Pallas kernels for 1% -> 2%
where the time goes in v5:
time: 252 us; the launch traced here: 251 us
  waiting for transfers between devices  109 us (43%)
  starting transfers between devices  89.6 us (36%)
  blocking collectives  36.7 us (15%)
  Pallas kernels  9.8 us (4%)
  local copies, waits for them, and re-layouts  4.1 us (2%)
    ppermute x1, waiting for transfers between devices, per_device(): low = lax.ppermute(papers[pap_rows - RIM:], 'dev', forward)  56.7 us
    all_gather x1, blocking collectives, reduce_weight(): every = lax.all_gather(part, 'dev', axis_index_groups=ring, axis=0)  36.7 us
    all_to_all x1, starting transfers between devices, per_device(): arrived = lax.all_to_all(outgoing, 'dev', 0, 0, tiled=True)  30.4 us
    ppermute x7, starting transfers between devices, shift_sum(): lax.ppermute(piece(lax.rem(place + k, count)), axis, perm(k))  21.3 us
    all_to_all x1, waiting for transfers between devices, per_device(): arrived = lax.all_to_all(outgoing, 'dev', 0, 0, tiled=True)  15.7 us
    ppermute x2, starting transfers between devices, swap(): lax.ppermute(block, 'dev', [(d, d ^ step) for d in range(lax.axis_size('d...  14.3 us
    ppermute x7, waiting for transfers between devices, shift_sum(): lax.ppermute(piece(lax.rem(place + k, count)), axis, perm(k))  9.19 us
    ppermute x1, waiting for transfers between devices, per_device(): high = lax.ppermute(papers[:RIM], 'dev', backward)  8.87 us
  transfers between devices with their start and end apart: 15, of which 12 were waited for; matrix products, arithmetic and copies ran while one was open for 0% of the time, Pallas kernels for 2%

profile of v5, /device:TPU:1, one launch (start us, length us, event | category | flops | bytes accessed | tf_op | source)
XLA Modules:
  0.0 250.8 jit_solution(10346079689874342052)
XLA Ops:
  2.4 1.6 shard_map.130
  4.0 30.4 %all-to-all-start = ((bf16[64,2,3200]{2,1,0:T(2,128)(2,1)}), bf16[64,2,3200]{2,1,0:T(2,128)(2,1)S(1)}, u32[]{:S(2)}, u32[]{:S(2)}) async-start(bf16[64,2,3200]{2,1,0:T(2,128)(2,1)} %shard_map.130), calls=%async_computation | async-start | bytes 1638400 | tf_op jit(solution)/shard_map/all_to_all | solution.py:279
  34.5 3.7 %collective-permute-start = (bf16[64,768]{1,0:T(8,128)(2,1)S(1)}, bf16[64,768]{1,0:T(8,128)(2,1)S(1)}, u32[]{:S(2)}, u32[]{:S(2)}) collective-permute-start(bf16[64,768]{1,0:T(8,128)(2,1)S(1)} %get-tuple-element.27), channel_id=1, source_target_pairs={{0,1},{1,2},{2,3},{3,4},{4,5},{5,6},{6,7},{7,8},{8,9},{9,10},{10,1... | collective-permute-start | bytes 294920 | tf_op jit(solution)/shard_map/ppermute | solution.py:284
  38.2 1.9 collective-permute-start.1
  40.1 56.7 %collective-permute-done.low = bf16[64,768]{1,0:T(8,128)(2,1)S(1)} collective-permute-done((bf16[64,768]{1,0:T(8,128)(2,1)S(1)}, bf16[64,768]{1,0:T(8,128)(2,1)S(1)}, u32[]{:S(2)}, u32[]{:S(2)}) %collective-permute-start) | collective-permute-done | bytes 98336 | tf_op jit(solution)/shard_map/ppermute | solution.py:284
  96.7 8.9 %collective-permute-done.1.high = bf16[64,768]{1,0:T(8,128)(2,1)S(1)} collective-permute-done((bf16[64,768]{1,0:T(8,128)(2,1)S(1)}, bf16[64,768]{1,0:T(8,128)(2,1)S(1)}, u32[]{:S(2)}, u32[]{:S(2)}) %collective-permute-start.1) | collective-permute-done | bytes 98336 | tf_op jit(solution)/shard_map/ppermute | solution.py:285
  105.6 1.4 shard_map.131
  107.9 15.7 %all-to-all-done.arrived = bf16[64,2,3200]{2,1,0:T(2,128)(2,1)S(1)} async-done(((bf16[64,2,3200]{2,1,0:T(2,128)(2,1)}), bf16[64,2,3200]{2,1,0:T(2,128)(2,1)S(1)}, u32[]{:S(2)}, u32[]{:S(2)}) %all-to-all-start) | async-done | bytes 819232 | tf_op jit(solution)/shard_map/all_to_all | solution.py:279
  125.8 2.6 %shard_map.132 = (bf16[256,512]{1,0:T(8,128)(2,1)}, bf16[512,512]{1,0:T(8,128)(2,1)}, bf16[512,768]{1,0:T(8,128)(2,1)S(1)}, bf16[512,512]{1,0:T(8,128)(2,1)S(1)}) custom-call(bf16[64,2,3200]{2,1,0:T(2,128)(2,1)S(1)} %all-to-all-done.arrived, f32[256,512]{1,0:T(8,128)S(1)} %copy-done.9, bf16[256,512]{1,0:T(8,128)(2,1)S(1)} %copy-done.10, ...), custom_call_target="tpu_custom_call" | custom-call | flops 671088640 | bytes 4489216 | tf_op jit(solution)/shard_map/pallas_call | solution.py:36
  128.4 8.1 %all-to-all-start.1 = ((bf16[64,8,512]{2,1,0:T(8,128)(2,1)}), bf16[64,8,512]{2,1,0:T(8,128)(2,1)S(1)}, u32[]{:S(2)}, u32[]{:S(2)}) async-start(bf16[64,8,512]{2,1,0:T(8,128)(2,1)} %bitcast.7), calls=%async_computation.1 | async-start | bytes 1048576 | tf_op jit(solution)/shard_map/all_to_all | solution.py:303
  137.1 2.4 collective-permute-start.2
  140.9 4.5 %collective-permute-start.5 = (bf16[96,512]{1,0:T(8,128)(2,1)S(1)}, bf16[96,512]{1,0:T(8,128)(2,1)S(1)}, u32[]{:S(2)}, u32[]{:S(2)}) collective-permute-start(bf16[96,512]{1,0:T(8,128)(2,1)S(1)} %get-tuple-element.24), channel_id=1, source_target_pairs={{0,768},{64,832},{128,896},{192,960},{256,0},{320,64},{384,128},{4... | collective-permute-start | bytes 294920 | tf_op jit(solution)/shard_map/ppermute | solution.py:175
  145.5 2.4 collective-permute-start.4
  147.9 2.5 %collective-permute-start.3 = (bf16[96,512]{1,0:T(8,128)(2,1)S(1)}, bf16[96,512]{1,0:T(8,128)(2,1)S(1)}, u32[]{:S(2)}, u32[]{:S(2)}) collective-permute-start(bf16[96,512]{1,0:T(8,128)(2,1)S(1)} %get-tuple-element.23), channel_id=1, source_target_pairs={{0,256},{64,320},{128,384},{192,448},{256,512},{320,576},{384,640}... | collective-permute-start | bytes 294920 | tf_op jit(solution)/shard_map/ppermute | solution.py:175
  150.5 2.2 collective-permute-done.4
  152.6 2.3 collective-permute-done.3
  155.0 4.6 %collective-permute-start.8 = (bf16[24,512]{1,0:T(8,128)(2,1)S(1)}, bf16[24,512]{1,0:T(8,128)(2,1)S(1)}, u32[]{:S(2)}, u32[]{:S(2)}) collective-permute-start(bf16[24,512]{1,0:T(8,128)(2,1)S(1)} %get-tuple-element.29), channel_id=1, source_target_pairs={{0,192},{64,0},{128,64},{192,128},{256,448},{320,256},{384,320},{4... | collective-permute-start | bytes 73736 | tf_op jit(solution)/shard_map/ppermute | solution.py:175
  159.7 2.3 collective-permute-start.7
  161.9 2.6 %collective-permute-start.6 = (bf16[24,512]{1,0:T(8,128)(2,1)S(1)}, bf16[24,512]{1,0:T(8,128)(2,1)S(1)}, u32[]{:S(2)}, u32[]{:S(2)}) collective-permute-start(bf16[24,512]{1,0:T(8,128)(2,1)S(1)} %get-tuple-element.28), channel_id=1, source_target_pairs={{0,64},{64,128},{128,192},{192,0},{256,320},{320,384},{384,448},{4... | collective-permute-start | bytes 73736 | tf_op jit(solution)/shard_map/ppermute | solution.py:175
  164.6 1.5 collective-permute-done.7
  166.0 2.0 collective-permute-done.6
  168.0 3.2 %collective-permute-start.9 = (f32[24,256]{1,0:T(8,128)S(1)}, f32[24,256]{1,0:T(8,128)S(1)}, u32[]{:S(2)}, u32[]{:S(2)}) collective-permute-start(f32[24,256]{1,0:T(8,128)S(1)} %constant_dynamic-slice_fusion), channel_id=1, source_target_pairs={{0,2},{1,3},{2,0},{3,1},{4,6},{5,7},{6,4},{7,5},{8,10},{9,11},{10,... | collective-permute-start | bytes 73736 | tf_op jit(solution)/shard_map/ppermute | solution.py:191
  171.2 7.9 %collective-permute-done.9 = f32[24,256]{1,0:T(8,128)S(1)} collective-permute-done((f32[24,256]{1,0:T(8,128)S(1)}, f32[24,256]{1,0:T(8,128)S(1)}, u32[]{:S(2)}, u32[]{:S(2)}) %collective-permute-start.9) | collective-permute-done | bytes 24608 | tf_op jit(solution)/shard_map/ppermute | solution.py:191
  179.2 36.7 %all-gather = bf16[384,256]{1,0:T(8,128)(2,1)S(1)} all-gather(bf16[24,256]{1,0:T(8,128)(2,1)S(1)} %add_convert_fusion.2), channel_id=2, replica_groups={{0,4,8,12,16,20,24,28,32,36,40,44,48,52,56,60},{1,5,9,13,17,21,25,29,33..., dimensions={0}, use_global_device_ids=true | all-gather | bytes 208896 | tf_op jit(solution)/shard_map/all_gather | solution.py:230
  215.9 2.1 collective-permute-start.10
  218.0 2.3 collective-permute-done.10.other
  221.1 6.8 %all-to-all-start.2 = ((bf16[16,24,512]{2,1,0:T(8,128)(2,1)}), bf16[16,24,512]{2,1,0:T(8,128)(2,1)S(1)}, u32[]{:S(2)}, u32[]{:S(2)}) async-start(bf16[16,24,512]{2,1,0:T(8,128)(2,1)} %shard_map.135), calls=%async_computation.2 | async-start | bytes 786432 | tf_op jit(solution)/shard_map/all_to_all | solution.py:314
  227.9 1.4 shard_map.136
  229.3 6.6 %all-to-all-done.2 = bf16[16,24,512]{2,1,0:T(8,128)(2,1)S(1)} async-done(((bf16[16,24,512]{2,1,0:T(8,128)(2,1)}), bf16[16,24,512]{2,1,0:T(8,128)(2,1)S(1)}, u32[]{:S(2)}, u32[]{:S(2)}) %all-to-all-start.2) | async-done | bytes 393248 | tf_op jit(solution)/shard_map/all_to_all | solution.py:314
  235.9 12.2 %collective-permute-start.11 = (bf16[384,512]{1,0:T(8,128)(2,1)S(1)}, bf16[384,512]{1,0:T(8,128)(2,1)S(1)}, u32[]{:S(2)}, u32[]{:S(2)}) collective-permute-start(bf16[384,512]{1,0:T(8,128)(2,1)S(1)} %bitcast.12), channel_id=1, source_target_pairs={{0,1},{1,0},{2,3},{3,2},{4,5},{5,4},{6,7},{7,6},{8,9},{9,8},{10,11... | collective-permute-start | bytes 1179656 | tf_op jit(solution)/shard_map/ppermute | solution.py:196
  248.1 1.3 collective-permute-done.11.other
  249.4 1.4 shard_map.137
  (39 shorter events, 7.8 us)
Async XLA Ops:
  0.6 33.8 %copy-start = (bf16[256,768]{1,0:T(8,128)(2,1)S(1)}, bf16[256,768]{1,0:T(8,128)(2,1)}, u32[]{:S(2)}) copy-start(bf16[256,768]{1,0:T(8,128)(2,1)} %papers.1) | copy-start | bytes 1179652
  1.4 1.0 copy-start.5
  2.4 103.2 %copy-start.1 = (bf16[768,512]{1,0:T(8,128)(2,1)S(1)}, bf16[768,512]{1,0:T(8,128)(2,1)}, u32[]{:S(2)}) copy-start(bf16[768,512]{1,0:T(8,128)(2,1)} %w_self.1) | copy-start | bytes 2359300
  2.4 103.2 %copy-start.2 = (bf16[768,512]{1,0:T(8,128)(2,1)S(1)}, bf16[768,512]{1,0:T(8,128)(2,1)}, u32[]{:S(2)}) copy-start(bf16[768,512]{1,0:T(8,128)(2,1)} %w_cite.1) | copy-start | bytes 2359300
  2.4 103.2 %copy-start.6 = (s32[256,8]{0,1:T(8,128)S(1)}, s32[256,8]{0,1:T(8,128)}, u32[]{:S(2)}) copy-start(s32[256,8]{0,1:T(8,128)} %param.18) | copy-start | bytes 24580
  2.4 103.2 %copy-start.7 = (f32[512]{0:T(512)S(1)}, f32[512]{0:T(512)}, u32[]{:S(2)}) copy-start(f32[512]{0:T(512)} %param.17) | copy-start | bytes 6148
  4.0 119.6 %all-to-all-start = ((bf16[64,2,3200]{2,1,0:T(2,128)(2,1)}), bf16[64,2,3200]{2,1,0:T(2,128)(2,1)S(1)}, u32[]{:S(2)}, u32[]{:S(2)}) async-start(bf16[64,2,3200]{2,1,0:T(2,128)(2,1)} %shard_map.130), calls=%async_computation | async-start | bytes 1638400 | tf_op jit(solution)/shard_map/all_to_all | solution.py:279
  34.4 89.1 %copy-start.10 = (bf16[256,512]{1,0:T(8,128)(2,1)S(1)}, bf16[256,512]{1,0:T(8,128)(2,1)}, u32[]{:S(2)}) copy-start(bf16[256,512]{1,0:T(8,128)(2,1)} %cotangent.1) | copy-start | bytes 786436
  34.5 62.3 %collective-permute-start = (bf16[64,768]{1,0:T(8,128)(2,1)S(1)}, bf16[64,768]{1,0:T(8,128)(2,1)S(1)}, u32[]{:S(2)}, u32[]{:S(2)}) collective-permute-start(bf16[64,768]{1,0:T(8,128)(2,1)S(1)} %get-tuple-element.27), channel_id=1, source_target_pairs={{0,1},{1,2},{2,3},{3,4},{4,5},{5,6},{6,7},{7,8},{8,9},{9,10},{10,1... | collective-permute-start | bytes 294920 | tf_op jit(solution)/shard_map/ppermute | solution.py:284
  38.2 67.5 %collective-permute-start.1 = (bf16[64,768]{1,0:T(8,128)(2,1)S(1)}, bf16[64,768]{1,0:T(8,128)(2,1)S(1)}, u32[]{:S(2)}, u32[]{:S(2)}) collective-permute-start(bf16[64,768]{1,0:T(8,128)(2,1)S(1)} %get-tuple-element.26), channel_id=1, source_target_pairs={{1,0},{2,1},{3,2},{4,3},{5,4},{6,5},{7,6},{8,7},{9,8},{10,9},{11,1... | collective-permute-start | bytes 294920 | tf_op jit(solution)/shard_map/ppermute | solution.py:285
  107.1 0.8 copy-start.8
  123.6 1.1 copy-start.3
  124.7 1.0 copy-start.9
  128.4 92.8 %all-to-all-start.1 = ((bf16[64,8,512]{2,1,0:T(8,128)(2,1)}), bf16[64,8,512]{2,1,0:T(8,128)(2,1)S(1)}, u32[]{:S(2)}, u32[]{:S(2)}) async-start(bf16[64,8,512]{2,1,0:T(8,128)(2,1)} %bitcast.7), calls=%async_computation.1 | async-start | bytes 1048576 | tf_op jit(solution)/shard_map/all_to_all | solution.py:303
  137.1 3.7 %collective-permute-start.2 = (bf16[384,512]{1,0:T(8,128)(2,1)S(1)}, bf16[384,512]{1,0:T(8,128)(2,1)S(1)}, u32[]{:S(2)}, u32[]{:S(2)}) collective-permute-start(bf16[384,512]{1,0:T(8,128)(2,1)S(1)} %constant_dynamic-slice_fusion.7), channel_id=1, source_target_pairs={{0,1},{1,0},{2,3},{3,2},{4,5},{5,4},{6,7},{7,6},{8,9},{9,8},{10,11... | collective-permute-start | bytes 1179656 | tf_op jit(solution)/shard_map/ppermute | solution.py:175
  140.9 87.0 %copy-start.4 = (bf16[768,512]{1,0:T(8,128)(2,1)S(1)}, bf16[768,512]{1,0:T(8,128)(2,1)}, u32[]{:S(2)}) copy-start(bf16[768,512]{1,0:T(8,128)(2,1)} %w_aut.3) | copy-start | bytes 2359300
  140.9 9.5 %collective-permute-start.5 = (bf16[96,512]{1,0:T(8,128)(2,1)S(1)}, bf16[96,512]{1,0:T(8,128)(2,1)S(1)}, u32[]{:S(2)}, u32[]{:S(2)}) collective-permute-start(bf16[96,512]{1,0:T(8,128)(2,1)S(1)} %get-tuple-element.24), channel_id=1, source_target_pairs={{0,768},{64,832},{128,896},{192,960},{256,0},{320,64},{384,128},{4... | collective-permute-start | bytes 294920 | tf_op jit(solution)/shard_map/ppermute | solution.py:175
  145.5 7.2 %collective-permute-start.4 = (bf16[96,512]{1,0:T(8,128)(2,1)S(1)}, bf16[96,512]{1,0:T(8,128)(2,1)S(1)}, u32[]{:S(2)}, u32[]{:S(2)}) collective-permute-start(bf16[96,512]{1,0:T(8,128)(2,1)S(1)} %get-tuple-element.25), channel_id=1, source_target_pairs={{0,512},{64,576},{128,640},{192,704},{256,768},{320,832},{384,896}... | collective-permute-start | bytes 294920 | tf_op jit(solution)/shard_map/ppermute | solution.py:175
  147.9 7.0 %collective-permute-start.3 = (bf16[96,512]{1,0:T(8,128)(2,1)S(1)}, bf16[96,512]{1,0:T(8,128)(2,1)S(1)}, u32[]{:S(2)}, u32[]{:S(2)}) collective-permute-start(bf16[96,512]{1,0:T(8,128)(2,1)S(1)} %get-tuple-element.23), channel_id=1, source_target_pairs={{0,256},{64,320},{128,384},{192,448},{256,512},{320,576},{384,640}... | collective-permute-start | bytes 294920 | tf_op jit(solution)/shard_map/ppermute | solution.py:175
  155.0 9.5 %collective-permute-start.8 = (bf16[24,512]{1,0:T(8,128)(2,1)S(1)}, bf16[24,512]{1,0:T(8,128)(2,1)S(1)}, u32[]{:S(2)}, u32[]{:S(2)}) collective-permute-start(bf16[24,512]{1,0:T(8,128)(2,1)S(1)} %get-tuple-element.29), channel_id=1, source_target_pairs={{0,192},{64,0},{128,64},{192,128},{256,448},{320,256},{384,320},{4... | collective-permute-start | bytes 73736 | tf_op jit(solution)/shard_map/ppermute | solution.py:175
  159.7 6.4 %collective-permute-start.7 = (bf16[24,512]{1,0:T(8,128)(2,1)S(1)}, bf16[24,512]{1,0:T(8,128)(2,1)S(1)}, u32[]{:S(2)}, u32[]{:S(2)}) collective-permute-start(bf16[24,512]{1,0:T(8,128)(2,1)S(1)} %get-tuple-element.30), channel_id=1, source_target_pairs={{0,128},{64,192},{128,0},{192,64},{256,384},{320,448},{384,256},{4... | collective-permute-start | bytes 73736 | tf_op jit(solution)/shard_map/ppermute | solution.py:175
  161.9 6.1 %collective-permute-start.6 = (bf16[24,512]{1,0:T(8,128)(2,1)S(1)}, bf16[24,512]{1,0:T(8,128)(2,1)S(1)}, u32[]{:S(2)}, u32[]{:S(2)}) collective-permute-start(bf16[24,512]{1,0:T(8,128)(2,1)S(1)} %get-tuple-element.28), channel_id=1, source_target_pairs={{0,64},{64,128},{128,192},{192,0},{256,320},{320,384},{384,448},{4... | collective-permute-start | bytes 73736 | tf_op jit(solution)/shard_map/ppermute | solution.py:175
  168.0 11.1 %collective-permute-start.9 = (f32[24,256]{1,0:T(8,128)S(1)}, f32[24,256]{1,0:T(8,128)S(1)}, u32[]{:S(2)}, u32[]{:S(2)}) collective-permute-start(f32[24,256]{1,0:T(8,128)S(1)} %constant_dynamic-slice_fusion), channel_id=1, source_target_pairs={{0,2},{1,3},{2,0},{3,1},{4,6},{5,7},{6,4},{7,5},{8,10},{9,11},{10,... | collective-permute-start | bytes 73736 | tf_op jit(solution)/shard_map/ppermute | solution.py:191
  215.9 4.4 %collective-permute-start.10 = (bf16[24,256]{1,0:T(8,128)(2,1)S(1)}, bf16[24,256]{1,0:T(8,128)(2,1)S(1)}, u32[]{:S(2)}, u32[]{:S(2)}) collective-permute-start(bf16[24,256]{1,0:T(8,128)(2,1)S(1)} %shard_map.134.own), channel_id=1, source_target_pairs={{0,2},{1,3},{2,0},{3,1},{4,6},{5,7},{6,4},{7,5},{8,10},{9,11},{10,... | collective-permute-start | bytes 36872 | tf_op jit(solution)/shard_map/ppermute | solution.py:196
  221.1 14.7 %all-to-all-start.2 = ((bf16[16,24,512]{2,1,0:T(8,128)(2,1)}), bf16[16,24,512]{2,1,0:T(8,128)(2,1)S(1)}, u32[]{:S(2)}, u32[]{:S(2)}) async-start(bf16[16,24,512]{2,1,0:T(8,128)(2,1)} %shard_map.135), calls=%async_computation.2 | async-start | bytes 786432 | tf_op jit(solution)/shard_map/all_to_all | solution.py:314
  235.9 13.6 %collective-permute-start.11 = (bf16[384,512]{1,0:T(8,128)(2,1)S(1)}, bf16[384,512]{1,0:T(8,128)(2,1)S(1)}, u32[]{:S(2)}, u32[]{:S(2)}) collective-permute-start(bf16[384,512]{1,0:T(8,128)(2,1)S(1)} %bitcast.12), channel_id=1, source_target_pairs={{0,1},{1,0},{2,3},{3,2},{4,5},{5,4},{6,7},{7,6},{8,9},{9,8},{10,11... | collective-permute-start | bytes 1179656 | tf_op jit(solution)/shard_map/ppermute | solution.py:196
